TPU v7x, 128 devices: a whole 4x4x4 slice. The times are simulated.
128 devices in a mesh: ta: 32 (over y, x, core), gx: 4 (over z).
Axes of the slice: x: 4, y: 4, z: 4, core: 2. Of those that a mesh axis runs over, the one named last changes fastest.
Arguments:
- field: float32 [2, 512, 8, 16384], P(None, 'gx', None, 'ta'), may hold values from -6 to 6
- ion_rate: float32 [512, 8], P('gx'), may hold values from 3.0517578e-05 to 0.00048828125
- diffraction: float32 [16384], replicated, may hold values from 0.02 to 0.2
- coupling: float32 [16384], replicated, may hold values from 0.1 to 1
Outputs:
- spectrum: float32 [2, 512, 8, 16384], P(None, ('gx', 'ta'))
All inputs are finite; a program needn't handle non-finite values.
Results may differ from a plain program's by a relative error of at most 0.00017.
Values sent between devices are 32-bit elements; how exact they have to be, the bound alone decides.
A program may use at most 128 MiB of HBM per device.

v0:
```python
import math

import jax
import jax.numpy as jnp
from jax import lax
from jax.sharding import PartitionSpec as P

BARRIER = 2.0
KERR = 0.5
HIGH = lax.Precision.HIGHEST


def extended(x, sides, width):
    for axis, dim in sides:
        count, length = (lax.axis_size(axis), x.shape[dim])
        up = [(i, (i + 1) % count) for i in range(count - 1)]
        down = [(j, i) for i, j in up]
        last = lax.slice_in_dim(x, length - width, length, axis=dim)
        leading = lax.slice_in_dim(x, 0, width, axis=dim)
        before = lax.ppermute(last, axis, up)
        after = lax.ppermute(leading, axis, down)
        x = jnp.concatenate([before, x, after], axis=dim)
    return x


def second_diff(padded, axis, count):

    def window(offset):
        return lax.slice_in_dim(padded, offset, offset + count, axis=axis)

    return (-window(0) + 16.0 * window(1) - 30.0 * window(2) + 16.0 * window(3) - window(4)) / 12.0


def phase_table(rows, cols, modulus):
    left = lax.broadcasted_iota(jnp.int32, (rows, cols), 0)
    right = lax.broadcasted_iota(jnp.int32, (rows, cols), 1)
    angle = -2.0 * math.pi / modulus * (left * right % modulus).astype(jnp.float32)
    return (jnp.cos(angle), jnp.sin(angle))


def transform(real_part, imag_part):
    n_total = real_part.shape[-1]
    first = 1 << (n_total.bit_length() - 1) // 2
    second = n_total // first
    lead = real_part.shape[:-1]
    real_grid = real_part.reshape(lead + (first, second))
    imag_grid = imag_part.reshape(lead + (first, second))
    outer_cos, outer_sin = phase_table(first, first, first)
    section_re = jnp.einsum("...ab,ka->...kb", real_grid, outer_cos, precision=HIGH) - jnp.einsum(
        "...ab,ka->...kb", imag_grid, outer_sin, precision=HIGH
    )
    section_im = jnp.einsum("...ab,ka->...kb", real_grid, outer_sin, precision=HIGH) + jnp.einsum(
        "...ab,ka->...kb", imag_grid, outer_cos, precision=HIGH
    )
    twist_cos, twist_sin = phase_table(first, second, n_total)
    turned_re = section_re * twist_cos - section_im * twist_sin
    turned_im = section_re * twist_sin + section_im * twist_cos
    inner_cos, inner_sin = phase_table(second, second, second)
    final_re = jnp.einsum("...kb,mb->...mk", turned_re, inner_cos, precision=HIGH) - jnp.einsum(
        "...kb,mb->...mk", turned_im, inner_sin, precision=HIGH
    )
    final_im = jnp.einsum("...kb,mb->...mk", turned_re, inner_sin, precision=HIGH) + jnp.einsum(
        "...kb,mb->...mk", turned_im, inner_cos, precision=HIGH
    )
    return (final_re.reshape(lead + (n_total,)), final_im.reshape(lead + (n_total,)))


def on_device(field, ion_rate, diffraction, coupling):
    x_rows = field.shape[1]
    band = field.shape[2]
    t_block = field.shape[3]
    scale = 1.0 / math.sqrt(diffraction.shape[0])
    padded_x = extended(field, (("gx", 1),), 2)
    padded_y = jnp.pad(field, ((0, 0), (0, 0), (2, 2), (0, 0)))
    lap = second_diff(padded_x, 1, x_rows) + second_diff(padded_y, 2, band)
    real_part = field[0]
    imag_part = field[1]
    intensity = real_part * real_part + imag_part * imag_part
    rate = ion_rate[:, :, None] * jnp.exp(-BARRIER / jnp.sqrt(intensity + 1.0))
    row_index = lax.broadcasted_iota(jnp.int32, (t_block, t_block), 0)
    col_index = lax.broadcasted_iota(jnp.int32, (t_block, t_block), 1)
    upper = (row_index <= col_index).astype(jnp.float32)
    local_sum = jnp.dot(rate.reshape(-1, t_block), upper, precision=HIGH).reshape(rate.shape)
    totals = local_sum[:, :, -1]
    gathered = lax.all_gather(totals[None], "ta", axis=0, tiled=True)
    earlier = jnp.arange(gathered.shape[0], dtype=jnp.int32) < lax.axis_index("ta")
    offset = jnp.sum(jnp.where(earlier[:, None, None], gathered, 0.0), axis=0)
    integral = local_sum + offset[:, :, None]
    plasma = 1.0 - jnp.exp(-integral)
    nonlin = jnp.stack(
        [
            -KERR * intensity * imag_part - plasma * real_part,
            KERR * intensity * real_part - plasma * imag_part,
        ]
    )
    pieces = (
        lax.all_to_all(field, "ta", split_axis=1, concat_axis=3, tiled=True),
        lax.all_to_all(lap, "ta", split_axis=1, concat_axis=3, tiled=True),
        lax.all_to_all(nonlin, "ta", split_axis=1, concat_axis=3, tiled=True),
    )
    field_re, field_im = transform(pieces[0][0], pieces[0][1])
    lap_re, lap_im = transform(pieces[1][0], pieces[1][1])
    nonlin_re, nonlin_im = transform(pieces[2][0], pieces[2][1])
    out_re = (field_re - diffraction * lap_im - coupling * nonlin_im) * scale
    out_im = (field_im + diffraction * lap_re + coupling * nonlin_re) * scale
    return jnp.stack([out_re, out_im])


def solution(mesh):
    in_specs = (P(None, "gx", None, "ta"), P("gx", None), P(), P())
    out_specs = P(None, ("gx", "ta"), None, None)
    return jax.shard_map(
        on_device, mesh=mesh, in_specs=in_specs, out_specs=out_specs, check_vma=False
    )
```

profile of v0, /device:TPU:96, one launch (start us, length us, event | category | flops | bytes accessed | tf_op | source)
XLA Modules:
  0.0 314.9 jit_solution(2807449500595609083)
XLA Ops:
  0.0 2.7 fusion.231
  2.7 4.4 %fusion.36 = f32[128,8,512]{2,0,1:T(8,128)S(1)} fusion(f32[1,128,8,512]{3,2,1,0:T(8,128)S(1)} %get-tuple-element.18, f32[1,128,8,512]{3,2,1,0:T(8,128)S(1)} %get-tuple-element.17, f32[128,8]{0,1:T(8,128)S(1)} %copy-done.18), kind=kOutput, calls=%fused_computation.62 | convolution fusion | flops 3224633344 | bytes 6295552 | tf_op jit(solution)/shard_map/dot_general | solution.py:83
  8.5 54.9 %all-gather = f32[4096,8,1]{2,0,1:T(8,128)} all-gather(f32[128,8,1]{2,0,1:T(8,128)S(1)} %slice.97), channel_id=2, replica_groups=mesh['ta'=32,'gx'=4] {'ta'}, dimensions={0}, use_global_device_ids=true | all-gather | bytes 135168 | tf_op jit(solution)/shard_map/all_gather | solution.py:85
  63.4 9.7 %copy.29 = f32[4096,8,1]{0,1,2:T(8,128)S(1)} copy(f32[4096,8,1]{2,0,1:T(8,128)} %all-gather) | data formatting | bytes 262144 | tf_op jit(solution)/shard_map/all_gather | solution.py:85
  73.2 5.1 %subtract_bitcast_fusion.3 = (f32[1,128,8,512]{3,1,2,0:T(8,128)S(1)}, f32[1,128,8,512]{3,1,2,0:T(8,128)S(1)}) fusion(f32[1,128,8,512]{3,2,1,0:T(8,128)} %copy-done.13, f32[1,128,8,512]{3,2,1,0:T(8,128)S(1)} %get-tuple-element.17, f32[128,8,512]{2,0,1:T(8,128)} %copy-done.15, f32[128,8]{0,1:T(8,128)S(1)} %fusion.59), kind=kLoop, calls=%fused_computation.60 | loop fusion | flops 7340032 | bytes 10489856 | tf_op jit(solution)/shard_map/stack | solution.py:90
  78.9 4.4 %copy.30 = f32[2,128,8,512]{3,2,0,1:T(8,128)} copy(f32[2,128,8,512]{3,1,2,0:T(8,128)S(1)} %pad_maximum_fusion) | data formatting | bytes 8388608 | tf_op jit(solution)/shard_map/stack | solution.py:90
  83.3 4.9 %all-to-all-start.2 = ((f32[2,128,8,512]{3,2,0,1:T(8,128)}), f32[2,128,8,512]{3,2,0,1:T(8,128)}, u32[]{:S(2)}, u32[]{:S(2)}) async-start(f32[2,128,8,512]{3,2,0,1:T(8,128)} %copy.30), calls=%async_computation.2 | async-start | bytes 8388608 | tf_op jit(solution)/shard_map/all_to_all | solution.py:99
  90.4 4.5 %collective-permute-start.1 = (f32[2,2,8,512]{3,2,0,1:T(8,128)S(1)}, f32[2,2,8,512]{3,2,0,1:T(8,128)S(1)}, u32[]{:S(2)}, u32[]{:S(2)}) collective-permute-start(f32[2,2,8,512]{3,2,0,1:T(8,128)S(1)} %get-tuple-element.12), channel_id=1, source_target_pairs={{1,0},{2,1},{3,2},{5,4},{6,5},{7,6},{9,8},{10,9},{11,10},{13,12},{... | collective-permute-start | bytes 196616 | tf_op jit(solution)/shard_map/ppermute | solution.py:21
  94.9 4.8 %copy.18 = f32[2,128,8,512]{3,2,0,1:T(8,128)} copy(f32[2,128,8,512]{3,2,1,0:T(8,128)} %param.4) | data formatting | bytes 8388608 | tf_op args[0]
  100.7 41.0 %all-to-all-done.2 = f32[2,128,8,512]{3,2,0,1:T(8,128)} async-done(((f32[2,128,8,512]{3,2,0,1:T(8,128)}), f32[2,128,8,512]{3,2,0,1:T(8,128)}, u32[]{:S(2)}, u32[]{:S(2)}) %all-to-all-start.2) | async-done | bytes 4194336 | tf_op jit(solution)/shard_map/all_to_all | solution.py:99
  141.7 5.0 %all-to-all-start = ((f32[2,128,8,512]{3,2,0,1:T(8,128)}), f32[2,128,8,512]{3,2,0,1:T(8,128)}, u32[]{:S(2)}, u32[]{:S(2)}) async-start(f32[2,128,8,512]{3,2,0,1:T(8,128)} %copy.18), calls=%async_computation | async-start | bytes 8388608 | tf_op jit(solution)/shard_map/all_to_all | solution.py:97
  146.7 5.6 %constant_dynamic-update-slice_fusion = (f32[2,130,8,512]{3,2,0,1:T(8,128)}, f32[2,130,8,512]{3,2,0,1:T(8,128)S(1)}) fusion(f32[2,130,8,512]{3,2,0,1:T(8,128)} %constant_dynamic-update-slice_fusion.1, f32[2,128,8,512]{3,2,1,0:T(8,128)} %param.4), kind=kLoop, calls=%fused_computation.139 | loop fusion | bytes 12582912 | tf_op jit(solution)/shard_map/concatenate | solution.py:22
  152.3 7.0 %fusion.6 = f32[2,128,8,512]{3,2,0,1:T(8,128)} fusion(f32[2,128,8,512]{3,2,0,1:T(8,128)S(1)} %copy-done.7, f32[2,130,8,512]{3,2,0,1:T(8,128)S(1)} %constant_dynamic-update-slice_fusion.2, f32[2,130,8,512]{3,2,0,1:T(8,128)} %get-tuple-element.9), kind=kLoop, calls=%fused_computation.10 | loop fusion | flops 17825792 | bytes 25165824 | tf_op jit(solution)/shard_map/add | solution.py:75
  159.3 4.6 %copy.59 = f32[2,32,4,8,512]{4,1,3,2,0:T(8,128)S(1)} copy(f32[2,32,4,8,512]{4,3,0,2,1:T(8,128)} %bitcast.22) | data formatting | bytes 8388608 | tf_op jit(solution)/shard_map/all_to_all | solution.py:99
  163.9 2.5 fusion.230
  167.9 2.6 reshape_squeeze.23
  179.3 2.2 fusion.14
  181.5 4.1 %add_bitcast_fusion.1 = f32[4,8,128,128]{3,2,1,0:T(8,128)} fusion(f32[128,4,8,128]{3,0,2,1:T(8,128)S(1)} %fusion.14, f32[128,4,8,128]{3,0,2,1:T(8,128)S(1)} %convolution_add_fusion, f32[128,4,8,128]{3,0,2,1:T(8,128)S(1)} %convolution_subtract_fusion, f32[128,128]{1,0:T(8,128)S(1)} %get-tuple-element.21, f32[128,128]{1,0:T(8,128)S(1)} %get-tuple-element.22), kind=kOutput, calls=%fused_computation.56 | convolution fusion | flops 807632896 | bytes 8519680 | tf_op jit(solution)/shard_map/...kb,mb->...mk/dot_general | solution.py:62
  185.6 14.5 %all-to-all-done = f32[2,128,8,512]{3,2,0,1:T(8,128)} async-done(((f32[2,128,8,512]{3,2,0,1:T(8,128)}), f32[2,128,8,512]{3,2,0,1:T(8,128)}, u32[]{:S(2)}, u32[]{:S(2)}) %all-to-all-start) | async-done | bytes 4194336 | tf_op jit(solution)/shard_map/all_to_all | solution.py:97
  200.1 4.9 %all-to-all-start.1 = ((f32[2,128,8,512]{3,2,0,1:T(8,128)}), f32[2,128,8,512]{3,2,0,1:T(8,128)}, u32[]{:S(2)}, u32[]{:S(2)}) async-start(f32[2,128,8,512]{3,2,0,1:T(8,128)} %fusion.6), calls=%async_computation.1 | async-start | bytes 8388608 | tf_op jit(solution)/shard_map/all_to_all | solution.py:98
  205.0 4.6 %copy.61 = f32[2,32,4,8,512]{4,1,3,2,0:T(8,128)S(1)} copy(f32[2,32,4,8,512]{4,3,0,2,1:T(8,128)} %bitcast.3) | data formatting | bytes 8388608 | tf_op jit(solution)/shard_map/all_to_all | solution.py:97
  209.6 2.6 fusion.229
  212.1 2.8 reshape.152
  214.9 2.7 reshape_squeeze.18
  217.6 2.7 reshape_squeeze.19
  220.2 3.9 %fusion.76 = f32[128,4,8,128]{3,0,2,1:T(8,128)S(1)} fusion(f32[4,8,128,128]{3,2,1,0:T(8,128)} %reshape_squeeze.18), kind=kOutput, calls=%fused_computation.109 | convolution fusion | flops 805535744 | bytes 4194304 | tf_op jit(solution)/shard_map/...ab,ka->...kb/dot_general | solution.py:52
  232.9 3.9 %subtract_bitcast_fusion.4 = f32[4,8,128,128]{3,2,1,0:T(8,128)} fusion(f32[128,4,8,128]{3,0,2,1:T(8,128)S(1)} %fusion.30, f32[128,4,8,128]{3,0,2,1:T(8,128)S(1)} %convolution_add_fusion.2, f32[128,4,8,128]{3,0,2,1:T(8,128)S(1)} %convolution_subtract_fusion.2, f32[128,128]{1,0:T(8,128)S(1)} %get-tuple-element.21, f32[128,128]{1,0:T(8,128)S(1)} %get-tuple-element.22), kind=kOutput, calls=%fused_computation.72 | convolution fusion | flops 807632896 | bytes 8519680 | tf_op jit(solution)/shard_map/...kb,mb->...mk/dot_general | solution.py:59
  236.8 2.8 reshape.150
  239.6 4.0 %fusion.12 = f32[128,4,8,128]{3,0,2,1:T(8,128)S(1)} fusion(f32[128,4,8,128]{3,0,2,1:T(8,128)S(1)} %convolution_add_fusion, f32[128,4,8,128]{3,0,2,1:T(8,128)} %copy-done, f32[128,128]{1,0:T(8,128)S(1)} %get-tuple-element.21, f32[128,128]{1,0:T(8,128)S(1)} %get-tuple-element.22), kind=kOutput, calls=%fused_computation.27 | convolution fusion | flops 807108608 | bytes 6422528 | tf_op jit(solution)/shard_map/...kb,mb->...mk/dot_general | solution.py:59
  243.6 3.7 %subtract_bitcast_fusion = f32[4,8,128,128]{3,2,1,0:T(8,128)} fusion(f32[128,4,8,128]{3,0,2,1:T(8,128)S(1)} %fusion.12, f32[128,4,8,128]{3,0,2,1:T(8,128)S(1)} %convolution_add_fusion, f32[128,4,8,128]{3,0,2,1:T(8,128)S(1)} %copy-done.1, f32[128,128]{1,0:T(8,128)S(1)} %get-tuple-element.21, f32[128,128]{1,0:T(8,128)S(1)} %get-tuple-element.22), kind=kOutput, calls=%fused_computation.52 | convolution fusion | flops 807632896 | bytes 8519680 | tf_op jit(solution)/shard_map/...kb,mb->...mk/dot_general | solution.py:59
  247.3 2.9 reshape.155
  250.2 4.0 %fusion.28 = f32[128,4,8,128]{3,0,2,1:T(8,128)S(1)} fusion(f32[128,4,8,128]{3,0,2,1:T(8,128)S(1)} %copy-done.3, f32[128,4,8,128]{3,0,2,1:T(8,128)} %copy-done.4, f32[128,128]{1,0:T(8,128)S(1)} %get-tuple-element.21, f32[128,128]{1,0:T(8,128)S(1)} %get-tuple-element.22), kind=kOutput, calls=%fused_computation.43 | convolution fusion | flops 807108608 | bytes 6422528 | tf_op jit(solution)/shard_map/...kb,mb->...mk/dot_general | solution.py:62
  254.2 3.7 %add_bitcast_fusion = f32[4,8,128,128]{3,2,1,0:T(8,128)} fusion(f32[128,4,8,128]{3,0,2,1:T(8,128)S(1)} %fusion.28, f32[128,4,8,128]{3,0,2,1:T(8,128)S(1)} %copy-done.3, f32[128,4,8,128]{3,0,2,1:T(8,128)S(1)} %copy-done.5, f32[128,128]{1,0:T(8,128)S(1)} %get-tuple-element.21, f32[128,128]{1,0:T(8,128)S(1)} %get-tuple-element.22), kind=kOutput, calls=%fused_computation.54 | convolution fusion | flops 807632896 | bytes 8519680 | tf_op jit(solution)/shard_map/...kb,mb->...mk/dot_general | solution.py:62
  257.9 3.0 reshape.153
  260.8 4.6 %copy.60 = f32[2,32,4,8,512]{4,1,3,2,0:T(8,128)S(1)} copy(f32[2,32,4,8,512]{4,3,0,2,1:T(8,128)} %bitcast.11) | data formatting | bytes 8388608 | tf_op jit(solution)/shard_map/all_to_all | solution.py:98
  265.4 2.5 fusion.227
  269.6 3.5 %fusion.72 = f32[128,4,8,128]{3,0,2,1:T(8,128)} fusion(f32[4,8,128,128]{3,2,1,0:T(8,128)S(1)} %reshape_squeeze.20), kind=kOutput, calls=%fused_computation.105 | convolution fusion | flops 805535744 | bytes 4194304 | tf_op jit(solution)/shard_map/...ab,ka->...kb/dot_general | solution.py:52
  273.0 3.5 %fusion.88 = f32[128,4,8,128]{3,0,2,1:T(8,128)} fusion(f32[4,8,128,128]{3,2,1,0:T(8,128)S(1)} %reshape_squeeze.20), kind=kOutput, calls=%fused_computation.121 | convolution fusion | flops 805535744 | bytes 4194304 | tf_op jit(solution)/shard_map/...ab,ka->...kb/dot_general | solution.py:49
  276.5 2.8 reshape_squeeze.21
  279.4 4.5 %convolution_add_fusion.1 = f32[128,4,8,128]{3,0,2,1:T(8,128)S(1)} fusion(f32[128,4,8,128]{3,0,2,1:T(8,128)} %fusion.72, f32[4,8,128,128]{3,2,1,0:T(8,128)} %reshape_squeeze.21), kind=kOutput, calls=%fused_computation.77 | convolution fusion | flops 806060032 | bytes 6291456 | tf_op jit(solution)/shard_map/...ab,ka->...kb/dot_general | solution.py:52
  286.1 2.2 fusion.22
  288.3 3.6 %fusion.20 = f32[128,4,8,128]{3,0,2,1:T(8,128)} fusion(f32[128,4,8,128]{3,0,2,1:T(8,128)S(1)} %convolution_add_fusion.1, f32[128,4,8,128]{3,0,2,1:T(8,128)S(1)} %convolution_subtract_fusion.1, f32[128,128]{1,0:T(8,128)S(1)} %get-tuple-element.21, f32[128,128]{1,0:T(8,128)S(1)} %get-tuple-element.22), kind=kOutput, calls=%fused_computation.35 | convolution fusion | flops 807108608 | bytes 6422528 | tf_op jit(solution)/shard_map/...kb,mb->...mk/dot_general | solution.py:59
  291.9 3.7 %add_bitcast_fusion.2 = f32[4,8,128,128]{3,2,1,0:T(8,128)} fusion(f32[128,4,8,128]{3,0,2,1:T(8,128)S(1)} %fusion.22, f32[128,4,8,128]{3,0,2,1:T(8,128)S(1)} %convolution_add_fusion.1, f32[128,4,8,128]{3,0,2,1:T(8,128)S(1)} %convolution_subtract_fusion.1, f32[128,128]{1,0:T(8,128)S(1)} %get-tuple-element.21, f32[128,128]{1,0:T(8,128)S(1)} %get-tuple-element.22), kind=kOutput, calls=%fused_computation.69 | convolution fusion | flops 807632896 | bytes 8519680 | tf_op jit(solution)/shard_map/...kb,mb->...mk/dot_general | solution.py:62
  295.5 3.0 reshape.151
  298.6 5.8 %subtract_bitcast_fusion.1 = f32[4,8,128,128]{3,2,1,0:T(8,128)} fusion(f32[128,4,8,128]{3,0,2,1:T(8,128)} %fusion.20, f32[128,4,8,128]{3,0,2,1:T(8,128)S(1)} %convolution_add_fusion.1, f32[128,4,8,128]{3,0,2,1:T(8,128)} %copy-done.6, f32[128,128]{1,0:T(8,128)S(1)} %get-tuple-element.21, f32[128,128]{1,0:T(8,128)S(1)} %get-tuple-element.22), kind=kOutput, calls=%fused_computation.53 | convolution fusion | flops 807632896 | bytes 8519680 | tf_op jit(solution)/shard_map/...kb,mb->...mk/dot_general | solution.py:59
  304.4 2.9 reshape.154
  307.3 4.8 %subtract_multiply_fusion = (f32[1,4,8,16384]{3,2,1,0:T(8,128)S(1)}, f32[1,4,8,16384]{3,2,1,0:T(8,128)S(1)}) fusion(f32[1,4,8,16384]{3,2,1,0:T(8,128)S(1)} %copy-done.14, f32[1,4,8,16384]{3,2,1,0:T(8,128)} %reshape.150, f32[1,4,8,16384]{3,2,1,0:T(8,128)} %reshape.151, f32[16384]{0:T(1024)S(1)} %copy-done.16, f32[16384]{0:T(1024)S(1)} %copy-done.17, ...), kind=kLoop, calls=%fused_computation.55 | loop fusion | flops 5242880 | bytes 16908288 | tf_op jit(solution)/shard_map/mul | solution.py:104
  312.1 2.3 pad_maximum_fusion.1
  (61 shorter events, 27.9 us)
Async XLA Ops:
  0.0 2.7 copy-start.18
  2.7 4.5 %copy-start.13 = (f32[1,128,8,512]{3,2,1,0:T(8,128)}, f32[1,128,8,512]{3,2,1,0:T(8,128)S(1)}, u32[]{:S(2)}) copy-start(f32[1,128,8,512]{3,2,1,0:T(8,128)S(1)} %get-tuple-element.18) | copy-start | bytes 6291460
  7.1 1.4 copy-start.15
  83.3 58.3 %all-to-all-start.2 = ((f32[2,128,8,512]{3,2,0,1:T(8,128)}), f32[2,128,8,512]{3,2,0,1:T(8,128)}, u32[]{:S(2)}, u32[]{:S(2)}) async-start(f32[2,128,8,512]{3,2,0,1:T(8,128)} %copy.30), calls=%async_computation.2 | async-start | bytes 8388608 | tf_op jit(solution)/shard_map/all_to_all | solution.py:99
  89.1 11.0 %collective-permute-start = (f32[2,2,8,512]{3,2,0,1:T(8,128)S(1)}, f32[2,2,8,512]{3,2,0,1:T(8,128)S(1)}, u32[]{:S(2)}, u32[]{:S(2)}) collective-permute-start(f32[2,2,8,512]{3,2,0,1:T(8,128)S(1)} %get-tuple-element.11), channel_id=1, source_target_pairs={{0,1},{1,2},{2,3},{4,5},{5,6},{6,7},{8,9},{9,10},{10,11},{12,13},{... | collective-permute-start | bytes 196616 | tf_op jit(solution)/shard_map/ppermute | solution.py:20
  90.4 61.9 %collective-permute-start.1 = (f32[2,2,8,512]{3,2,0,1:T(8,128)S(1)}, f32[2,2,8,512]{3,2,0,1:T(8,128)S(1)}, u32[]{:S(2)}, u32[]{:S(2)}) collective-permute-start(f32[2,2,8,512]{3,2,0,1:T(8,128)S(1)} %get-tuple-element.12), channel_id=1, source_target_pairs={{1,0},{2,1},{3,2},{5,4},{6,5},{7,6},{9,8},{10,9},{11,10},{13,12},{... | collective-permute-start | bytes 196616 | tf_op jit(solution)/shard_map/ppermute | solution.py:21
  141.7 58.5 %all-to-all-start = ((f32[2,128,8,512]{3,2,0,1:T(8,128)}), f32[2,128,8,512]{3,2,0,1:T(8,128)}, u32[]{:S(2)}, u32[]{:S(2)}) async-start(f32[2,128,8,512]{3,2,0,1:T(8,128)} %copy.18), calls=%async_computation | async-start | bytes 8388608 | tf_op jit(solution)/shard_map/all_to_all | solution.py:97
  146.7 5.6 %copy-start.7 = (f32[2,128,8,512]{3,2,0,1:T(8,128)S(1)}, f32[2,128,8,512]{3,2,0,1:T(8,128)}, u32[]{:S(2)}) copy-start(f32[2,128,8,512]{3,2,0,1:T(8,128)} %copy.18) | copy-start | bytes 12582916
  172.7 2.2 copy-start.8
  179.2 2.3 copy-start
  200.1 60.7 %all-to-all-start.1 = ((f32[2,128,8,512]{3,2,0,1:T(8,128)}), f32[2,128,8,512]{3,2,0,1:T(8,128)}, u32[]{:S(2)}, u32[]{:S(2)}) async-start(f32[2,128,8,512]{3,2,0,1:T(8,128)} %fusion.6), calls=%async_computation.1 | async-start | bytes 8388608 | tf_op jit(solution)/shard_map/all_to_all | solution.py:98
  220.2 3.9 %copy-start.11 = (f32[4,8,128,128]{3,2,1,0:T(8,128)S(1)}, f32[4,8,128,128]{3,2,1,0:T(8,128)}, u32[]{:S(2)}) copy-start(f32[4,8,128,128]{3,2,1,0:T(8,128)} %reshape_squeeze.18) | copy-start | bytes 6291460
  224.1 2.2 copy-start.9
  228.5 4.4 %copy-start.2 = (f32[128,4,8,128]{3,0,2,1:T(8,128)}, f32[128,4,8,128]{3,0,2,1:T(8,128)S(1)}, u32[]{:S(2)}) copy-start(f32[128,4,8,128]{3,0,2,1:T(8,128)S(1)} %convolution_add_fusion.2) | copy-start | bytes 6291460
  230.6 2.3 copy-start.4
  239.6 4.0 %copy-start.1 = (f32[128,4,8,128]{3,0,2,1:T(8,128)S(1)}, f32[128,4,8,128]{3,0,2,1:T(8,128)}, u32[]{:S(2)}) copy-start(f32[128,4,8,128]{3,0,2,1:T(8,128)} %copy-done) | copy-start | bytes 6291460
  247.3 2.9 copy-start.3
  250.2 4.0 %copy-start.5 = (f32[128,4,8,128]{3,0,2,1:T(8,128)S(1)}, f32[128,4,8,128]{3,0,2,1:T(8,128)}, u32[]{:S(2)}) copy-start(f32[128,4,8,128]{3,0,2,1:T(8,128)} %copy-done.4) | copy-start | bytes 6291460
  279.4 4.5 %copy-start.10 = (f32[4,8,128,128]{3,2,1,0:T(8,128)S(1)}, f32[4,8,128,128]{3,2,1,0:T(8,128)}, u32[]{:S(2)}) copy-start(f32[4,8,128,128]{3,2,1,0:T(8,128)} %reshape_squeeze.21) | copy-start | bytes 6291460
  279.4 4.5 %copy-start.12 = (f32[128,4,8,128]{3,0,2,1:T(8,128)S(1)}, f32[128,4,8,128]{3,0,2,1:T(8,128)}, u32[]{:S(2)}) copy-start(f32[128,4,8,128]{3,0,2,1:T(8,128)} %fusion.88) | copy-start | bytes 6291460
  286.1 5.8 %copy-start.6 = (f32[128,4,8,128]{3,0,2,1:T(8,128)}, f32[128,4,8,128]{3,0,2,1:T(8,128)S(1)}, u32[]{:S(2)}) copy-start(f32[128,4,8,128]{3,0,2,1:T(8,128)S(1)} %convolution_subtract_fusion.1) | copy-start | bytes 6291460
  304.4 2.9 copy-start.14
  304.4 2.9 copy-start.16
  304.4 2.9 copy-start.17
where the time goes:
time: 321 us; the launch traced here: 315 us
  local copies, waits for them, and re-layouts  82.9 us (26%)
  matrix products  79.9 us (25%)
  waiting for transfers between devices  55.5 us (17%)
  blocking collectives  54.9 us (17%)
  starting transfers between devices  20.6 us (6%)
  other arithmetic  20.1 us (6%)
    all_gather x1, blocking collectives, on_device(): gathered = lax.all_gather(totals[None], 'ta', axis=0, tiled=True)  54.9 us
    all_to_all x1, waiting for transfers between devices, on_device(): lax.all_to_all(nonlin, 'ta', split_axis=1, concat_axis=3, tiled=True)  41 us
    all_to_all x1, waiting for transfers between devices, on_device(): lax.all_to_all(field, 'ta', split_axis=1, concat_axis=3, tiled=True)  14.5 us
    dot_general x3, matrix products, transform(): jnp.einsum('...kb,mb->...mk', turned_re, inner_cos, precision=HIGH)  13.3 us
    dot_general x3, matrix products, transform(): jnp.einsum('...kb,mb->...mk', turned_re, inner_sin, precision=HIGH)  11.4 us
    dot_general x3, matrix products, transform(): jnp.einsum('...kb,mb->...mk', turned_im, inner_sin, precision=HIGH)  9.75 us
    all_gather x1, local copies, waits for them, and re-layouts, on_device(): gathered = lax.all_gather(totals[None], 'ta', axis=0, tiled=True)  9.69 us
    dot_general x3, matrix products, transform(): jnp.einsum('...ab,ka->...kb', real_grid, outer_sin, precision=HIGH)  9.45 us
  transfers between devices with their start and end apart: 5, of which 2 were waited for; matrix products, arithmetic and copies ran while one was open for 32% of the time, Pallas kernels for 0%

commit v1 on v0

v1 whole, which is shorter than its diff:
```python
import math

import jax
import jax.numpy as jnp
import ml_dtypes
import numpy as np
from jax import lax
from jax.experimental import pallas as pl
from jax.experimental.pallas import tpu as pltpu
from jax.sharding import PartitionSpec as P

BARRIER = 2.0
KERR = 0.5
MESH = pl.DeviceIdType.MESH
R = 128
TA = 32
GX = 4
ROWS = 4
Y = 8
F32 = jnp.float32
BF16 = jnp.bfloat16


def tables():
    index = np.arange(R)
    angle = 2.0 * np.pi / R * (np.outer(index, index) % R)
    cos, sin = np.cos(angle), np.sin(angle)
    full = np.block([[cos, sin], [-sin, cos]]).astype(np.float32)
    high = full.astype(ml_dtypes.bfloat16)
    low = (full - high.astype(np.float32)).astype(ml_dtypes.bfloat16)
    dft = np.concatenate([high, low, high], axis=1)
    turn = 2.0 * np.pi / (R * R) * np.outer(index, index)
    twist = np.stack([np.cos(turn), -np.sin(turn)]) / R
    upper = (index[:, None] <= index[None, :]).astype(np.float32)
    within = np.concatenate([upper, np.ones((R, R), np.float32)], axis=1)
    within = np.concatenate([within, within], axis=0)
    lower = (index[:, None] > index[None, :]).astype(np.float32)
    before = np.concatenate([lower, lower], axis=1)
    return (
        dft,
        twist.astype(np.float32),
        within.astype(ml_dtypes.bfloat16),
        before.astype(ml_dtypes.bfloat16),
    )


def halves(v):
    high = v.astype(BF16)
    return high, (v - high.astype(F32)).astype(BF16)


def dot(a, b):
    return jnp.dot(a, b, preferred_element_type=F32)


def dot_nt(a, b):
    return lax.dot_general(a, b, (((1,), (1,)), ((), ())), preferred_element_type=F32)


def kernel(
    ion_ref, field, coupling_in, diffraction_in, dft_in, twist_in, within_in, before_in,
    out,
    rx, fe, part, result, coupling, diffraction, dft, twist, within, before,
    const_sem, send_sem, recv_sem, halo_send, halo_recv, out_sem,
):
    me = lax.axis_index("ta")
    g = lax.axis_index("gx")
    odd = lax.rem(me, 2)
    has_left = jnp.logical_or(me > 0, g > 0)
    has_right = jnp.logical_or(me < TA - 1, g < GX - 1)
    left_ta = lax.rem(me + TA - 1, TA)
    left_gx = lax.rem(jnp.where(me == 0, g + GX - 1, g), GX)
    right_ta = lax.rem(me + 1, TA)
    right_gx = lax.rem(jnp.where(me == TA - 1, g + 1, g), GX)

    def row_at(step, parity):
        return jnp.where(parity == 0, step, ROWS - 1 - step)

    gate = pltpu.get_barrier_semaphore()

    def greet(off, carry):
        pl.semaphore_signal(
            gate, inc=1, device_id=(lax.rem(me + off, TA), g), device_id_type=MESH
        )
        return carry

    lax.fori_loop(1, TA, greet, 0)
    pl.semaphore_signal(gate, inc=1, device_id=(left_ta, left_gx), device_id_type=MESH)
    pl.semaphore_signal(gate, inc=1, device_id=(right_ta, right_gx), device_id_type=MESH)
    pl.semaphore_wait(gate, TA + 1)

    constants = [
        pltpu.make_async_copy(src, dst, const_sem.at[n])
        for n, (src, dst) in enumerate(
            [
                (coupling_in, coupling),
                (diffraction_in, diffraction),
                (dft_in, dft),
                (twist_in, twist),
                (within_in, within),
                (before_in, before),
            ]
        )
    ]
    for copy in constants:
        copy.start()

    place = pl.ds(pl.multiple_of(me * 32, 32), 32)
    for step in range(ROWS):

        def send(off, carry, step=step):
            to = lax.rem(me + off, TA)
            row = row_at(step, lax.rem(to, 2))
            pltpu.make_async_remote_copy(
                src_ref=field.at[:, 4 * to + row],
                dst_ref=rx.at[row, :, place],
                send_sem=send_sem.at[step],
                recv_sem=recv_sem.at[step],
                device_id=(to, g),
                device_id_type=MESH,
            ).start()
            return carry

        lax.fori_loop(1, TA, send, 0)
        own = row_at(step, odd)
        pltpu.make_async_copy(
            field.at[:, 4 * me + own], rx.at[own, :, place], recv_sem.at[step]
        ).start()

    @pl.when(jnp.logical_not(has_left))
    def _():
        fe[0:2] = jnp.zeros((2, 2, Y * R, R), F32)

    @pl.when(jnp.logical_not(has_right))
    def _():
        fe[6:8] = jnp.zeros((2, 2, Y * R, R), F32)

    for copy in constants:
        copy.wait()

    def halo_copy(row, to_left):
        return pltpu.make_async_remote_copy(
            src_ref=fe.at[row + 2],
            dst_ref=fe.at[lax.rem(row + 6, 8)],
            send_sem=halo_send.at[row],
            recv_sem=halo_recv.at[row],
            device_id=(left_ta, left_gx) if to_left else (right_ta, right_gx),
            device_id_type=MESH,
        )

    def transform(groups):
        real = jnp.concatenate([re for re, _ in groups], axis=1)
        imag = jnp.concatenate([im for _, im in groups], axis=1)
        high, low = halves(jnp.concatenate([real, imag], axis=0))
        table = dft[...]
        section = dot(table, jnp.concatenate([high, high, low], axis=0))
        cos, sin = twist[0], twist[1]
        turned = []
        for n in range(len(groups)):
            re = section[:R, n * R : (n + 1) * R]
            im = section[R:, n * R : (n + 1) * R]
            turned.append(
                jnp.concatenate([re * cos - im * sin, re * sin + im * cos], axis=1)
            )
        high, low = halves(jnp.concatenate(turned, axis=0))
        final = dot_nt(table, jnp.concatenate([high, high, low], axis=1))
        return [
            (final[:R, n * R : (n + 1) * R], final[R:, n * R : (n + 1) * R])
            for n in range(len(groups))
        ]

    def pair(row, p):
        groups_e, groups_n = [], []
        for side in range(2):
            y = 2 * p + side
            re = rx[row, 0, pl.ds(y, R, stride=Y), :]
            im = rx[row, 1, pl.ds(y, R, stride=Y), :]
            intensity = re * re + im * im
            rate = ion_ref[4 * me + row, y] * jnp.exp(-BARRIER * lax.rsqrt(intensity + 1.0))
            sums = dot(jnp.concatenate(halves(rate), axis=1), within[...])
            earlier = dot(before[...], jnp.concatenate(halves(sums[:, R:]), axis=0))
            plasma = 1.0 - jnp.exp(-(sums[:, :R] + earlier))
            groups_e.append((re, im))
            kerr = KERR * intensity
            groups_n.append((-kerr * im - plasma * re, kerr * re - plasma * im))
        spectra = transform(groups_e + groups_n)
        c = coupling[...]
        for side in range(2):
            at = pl.ds(pl.multiple_of((2 * p + side) * R, R), R)
            e_re, e_im = spectra[side]
            n_re, n_im = spectra[2 + side]
            fe[row + 2, 0, at, :] = e_re
            fe[row + 2, 1, at, :] = e_im
            part[row, 0, at, :] = e_re - c * n_im
            part[row, 1, at, :] = e_im + c * n_re

    for step in range(ROWS):
        row = row_at(step, odd)
        pltpu.make_async_copy(rx.at[row], rx.at[row], recv_sem.at[step]).wait()

        def body(p, carry, row=row):
            pair(row, p)
            return carry

        lax.fori_loop(0, Y // 2, body, 0)

        @pl.when(jnp.logical_and(row < 2, has_left))
        def _(row=row):
            halo_copy(row, True).start()

        @pl.when(jnp.logical_and(row >= 2, has_right))
        def _(row=row):
            halo_copy(row, False).start()

    def arrived(row):
        pltpu.make_async_copy(
            fe.at[lax.rem(row + 6, 8)], fe.at[lax.rem(row + 6, 8)], halo_recv.at[row]
        ).wait()

    def left_arrived():
        @pl.when(has_left)
        def _():
            arrived(2)
            arrived(3)

    def right_arrived():
        @pl.when(has_right)
        def _():
            arrived(0)
            arrived(1)

    def finish(row):
        def block(n, carry):
            k = pl.multiple_of(n * 8, 8)
            d = diffraction[pl.ds(k, 8), :] * (1.0 / 12.0)
            lap = []
            for c in range(2):
                mid = [fe[row + 2, c, pl.ds(y * R + k, 8), :] for y in range(Y)]
                planes = []
                for y in range(Y):
                    at = pl.ds(y * R + k, 8)
                    near = fe[row + 1, c, at, :] + fe[row + 3, c, at, :]
                    far = fe[row, c, at, :] + fe[row + 4, c, at, :]
                    for o in (-1, 1):
                        if 0 <= y + o < Y:
                            near = near + mid[y + o]
                    for o in (-2, 2):
                        if 0 <= y + o < Y:
                            far = far + mid[y + o]
                    planes.append(16.0 * near - far - 60.0 * mid[y])
                lap.append(planes)
            for y in range(Y):
                at = pl.ds(y * R + k, 8)
                to = pl.ds(k * Y + y, 8, stride=Y)
                result[row, 0, to, :] = part[row, 0, at, :] - d * lap[1][y]
                result[row, 1, to, :] = part[row, 1, at, :] + d * lap[0][y]
            return carry

        lax.fori_loop(0, R // 8, block, 0)
        copy = pltpu.make_async_copy(result.at[row], out.at[:, row], out_sem.at[row])
        copy.start()

    @pl.when(odd == 0)
    def _():
        left_arrived()

    @pl.when(odd == 1)
    def _():
        right_arrived()

    for step in range(2):
        finish(row_at(step, odd))

    @pl.when(odd == 0)
    def _():
        right_arrived()

    @pl.when(odd == 1)
    def _():
        left_arrived()

    for step in range(2, ROWS):
        finish(row_at(step, odd))

    for row in range(ROWS):
        pltpu.make_async_copy(result.at[row], out.at[:, row], out_sem.at[row]).wait()
    for step in range(ROWS):
        sent = rx.at[0, :, pl.ds(0, (TA - 1) * 32)]
        pltpu.make_async_copy(sent, sent, send_sem.at[step]).wait()
    for row in range(ROWS):

        @pl.when(has_left if row < 2 else has_right)
        def _(row=row):
            halo_copy(row, row < 2).wait_send()


def on_device(field, ion_rate, diffraction, coupling):
    x_rows = field.shape[1]
    tiles = field.reshape(2, x_rows, Y, 4, R).transpose(0, 1, 3, 2, 4).reshape(2, x_rows, 32, R)
    dft, twist, within, before = tables()
    hbm = pl.BlockSpec(memory_space=pl.ANY)
    spectrum = pl.pallas_call(
        kernel,
        out_shape=jax.ShapeDtypeStruct((2, ROWS, R * Y, R), F32),
        in_specs=[pl.BlockSpec(memory_space=pltpu.SMEM)] + [hbm] * 7,
        out_specs=hbm,
        scratch_shapes=[
            pltpu.VMEM((ROWS, 2, R * Y, R), F32),
            pltpu.VMEM((ROWS + 4, 2, Y * R, R), F32),
            pltpu.VMEM((ROWS, 2, Y * R, R), F32),
            pltpu.VMEM((ROWS, 2, R * Y, R), F32),
            pltpu.VMEM((R, R), F32),
            pltpu.VMEM((R, R), F32),
            pltpu.VMEM(dft.shape, BF16),
            pltpu.VMEM(twist.shape, F32),
            pltpu.VMEM(within.shape, BF16),
            pltpu.VMEM(before.shape, BF16),
            pltpu.SemaphoreType.DMA((6,)),
            pltpu.SemaphoreType.DMA((ROWS,)),
            pltpu.SemaphoreType.DMA((ROWS,)),
            pltpu.SemaphoreType.DMA((ROWS,)),
            pltpu.SemaphoreType.DMA((ROWS,)),
            pltpu.SemaphoreType.DMA((ROWS,)),
        ],
        compiler_params=pltpu.CompilerParams(
            collective_id=0, has_side_effects=True, vmem_limit_bytes=48 * 1024 * 1024
        ),
    )(
        ion_rate,
        tiles,
        coupling.reshape(R, R),
        diffraction.reshape(R, R),
        jnp.asarray(dft),
        jnp.asarray(twist),
        jnp.asarray(within),
        jnp.asarray(before),
    )
    spectrum = spectrum.reshape(2, ROWS, R, Y, R).transpose(0, 1, 3, 2, 4)
    return spectrum.reshape(2, ROWS, Y, R * R)


def solution(mesh):
    in_specs = (P(None, "gx", None, "ta"), P("gx", None), P(), P())
    out_specs = P(None, ("gx", "ta"), None, None)
    return jax.shard_map(
        on_device, mesh=mesh, in_specs=in_specs, out_specs=out_specs, check_vma=False
    )
```

time: 321 us -> 94.3 us (0.29); the launches traced: 315 us -> 93.5 us
  Pallas kernels: 0 us -> 85.4 us
  matrix products: 79.9 us -> 0 us
  local copies, waits for them, and re-layouts: 82.9 us -> 8.12 us
  waiting for transfers between devices: 55.5 us -> 0 us
  blocking collectives: 54.9 us -> 0 us
  starting transfers between devices: 20.6 us -> 0 us
  other arithmetic: 20.1 us -> 0 us
    pallas_call x0 -> x1, Pallas kernels: none -> 85.4 us  [on_device(): pl.pallas_call(kernel, out_shape=jax.ShapeDtypeStruct((2, ROWS, R * Y, R)...]
    dot_general x25 -> x0, matrix products: 79.9 us -> none  [the longest x3 13.3 us: transform(): jnp.einsum('...kb,mb->...mk', turned_re, inner_cos, precision=HIGH)]
    all_to_all x3 -> x0, waiting for transfers between devices: 55.5 us -> none  [the longest x1 41 us: on_device(): lax.all_to_all(nonlin, 'ta', split_axis=1, concat_axis=3, tiled=True)]
    all_gather x1 -> x0, blocking collectives: 54.9 us -> none  [on_device(): gathered = lax.all_gather(totals[None], 'ta', axis=0, tiled=True)]
    another operation x7 -> x0, local copies, waits for them, and re-layouts: 18.4 us -> none  [the longest x3 8.1 us: transform(): imag_grid = imag_part.reshape(lead + (first, second))]
    reshape x6 -> x0, local copies, waits for them, and re-layouts: 17.4 us -> none  [the longest x3 8.8 us: transform(): final_im.reshape(lead + (n_total,))]
    all_to_all x3 -> x0, starting transfers between devices: 14.8 us -> none  [the longest x1 5.03 us: on_device(): lax.all_to_all(field, 'ta', split_axis=1, concat_axis=3, tiled=True)]
    all_to_all x3 -> x0, local copies, waits for them, and re-layouts: 13.7 us -> none  [the longest x1 4.56 us: on_device(): lax.all_to_all(field, 'ta', split_axis=1, concat_axis=3, tiled=True)]
  transfers between devices with their start and end apart: 5 -> 0, of which waited for: 2 -> 0; matrix products, arithmetic and copies ran while one was open for 32% -> 0% of each run, Pallas kernels for 0% -> 0%
where the time goes in v1:
time: 94.3 us; the launch traced here: 93.5 us
  Pallas kernels  85.4 us (91%)
  local copies, waits for them, and re-layouts  8.12 us (9%)
    pallas_call x1, Pallas kernels, on_device(): pl.pallas_call(kernel, out_shape=jax.ShapeDtypeStruct((2, ROWS, R * Y, R)...  85.4 us
    unnamed x14, local copies, waits for them, and re-layouts  8.12 us

profile of v1, /device:TPU:96, one launch (start us, length us, event | category | flops | bytes accessed | tf_op | source)
XLA Modules:
  0.0 93.5 jit_solution(9243194294359671306)
XLA Ops:
  0.0 0.8 copy.9.ion_ref
  0.8 0.0 copy-start
  0.8 1.0 %copy-done = bf16[256,768]{1,0:T(8,128)(2,1)S(1)} copy-done((bf16[256,768]{1,0:T(8,128)(2,1)S(1)}, bf16[256,768]{1,0:T(8,128)(2,1)}, u32[]{:S(2)}) %copy-start) | copy-done | bytes 393240
  1.8 0.0 copy-start.1
  1.8 0.9 copy-done.1
  2.7 0.0 copy-start.2
  2.7 0.9 copy-done.2
  3.6 0.0 copy-start.3
  3.6 0.8 copy-done.3
  4.4 0.0 copy-start.4
  4.4 0.8 copy-done.4
  5.3 0.0 copy-start.5
  5.3 0.8 copy-done.5
  6.1 85.4 %shard_map.82 = f32[2,4,1024,128]{3,2,1,0:T(8,128)S(1)} custom-call(f32[128,8]{1,0:T(8,128)S(1)} %copy.9.ion_ref, f32[2,128,32,128]{3,2,1,0:T(8,128)} %bitcast.15, f32[128,128]{1,0:T(8,128)S(1)} %bitcast.13, f32[128,128]{1,0:T(8,128)S(1)} %bitcast.14, bf16[256,768]{1,0:T(8,128)(2,1)S(1)} %copy-done, f32[2,128,128]{2,1,0:T(8,128)S(1)} %copy-done.2, ...), custom_call_target="tpu_custom_call" | custom-call | tf_op jit(solution)/shard_map/pallas_call | solution.py:302
  91.5 2.0 %copy.11 = f32[2,4,8,16384]{3,2,1,0:T(8,128)} copy(f32[2,4,8,16384]{3,2,1,0:T(8,128)S(1)} %bitcast.12) | data formatting | bytes 8388608
Async XLA Ops:
  0.8 1.0 %copy-start = (bf16[256,768]{1,0:T(8,128)(2,1)S(1)}, bf16[256,768]{1,0:T(8,128)(2,1)}, u32[]{:S(2)}) copy-start(bf16[256,768]{1,0:T(8,128)(2,1)} %constant.8.clone.dft_in) | copy-start | bytes 1179652
  1.8 0.9 copy-start.1
  2.7 0.9 copy-start.2
  3.6 0.8 copy-start.3
  4.4 0.8 copy-start.4
  5.3 0.8 copy-start.5

commit v2 on v1

v2 whole, which is shorter than its diff:
```python
import math

import jax
import jax.numpy as jnp
import ml_dtypes
import numpy as np
from jax import lax
from jax.experimental import pallas as pl
from jax.experimental.pallas import tpu as pltpu
from jax.sharding import PartitionSpec as P

BARRIER = 2.0
KERR = 0.5
MESH = pl.DeviceIdType.MESH
R = 128
TA = 32
GX = 4
LINES = 4
COLS = 4
ROWS = 4
Y = 8
F32 = jnp.float32
BF16 = jnp.bfloat16
INNER, OWN, NEAR, FAR, AHEAD, FORWARD = 0, 2, 4, 5, 6, 7


def tables():
    index = np.arange(R)
    angle = 2.0 * np.pi / R * (np.outer(index, index) % R)
    cos, sin = np.cos(angle), np.sin(angle)
    full = np.block([[cos, sin], [-sin, cos]]).astype(np.float32)
    high = full.astype(ml_dtypes.bfloat16)
    low = (full - high.astype(np.float32)).astype(ml_dtypes.bfloat16)
    dft = np.concatenate([high, low, high], axis=1)
    turn = 2.0 * np.pi / (R * R) * np.outer(index, index)
    twist = np.stack([np.cos(turn), -np.sin(turn)]) / R
    upper = (index[:, None] <= index[None, :]).astype(np.float32)
    within = np.concatenate([upper, np.ones((R, R), np.float32)], axis=1)
    within = np.concatenate([within, within], axis=0)
    lower = (index[:, None] > index[None, :]).astype(np.float32)
    before = np.concatenate([lower, lower], axis=1)
    return (
        dft,
        twist.astype(np.float32),
        within.astype(ml_dtypes.bfloat16),
        before.astype(ml_dtypes.bfloat16),
    )


def halves(v):
    high = v.astype(BF16)
    return high, (v - high.astype(F32)).astype(BF16)


def dot(a, b):
    return jnp.dot(a, b, preferred_element_type=F32)


def dot_nt(a, b):
    return lax.dot_general(a, b, (((1,), (1,)), ((), ())), preferred_element_type=F32)


def kernel(
    ion_in, field, coupling_in, diffraction_in, dft_in, twist_in, within_in, before_in,
    out,
    rx, fe, part, result, ion_ref, coupling, diffraction, dft, twist, within, before,
    const_sem, send_sem, recv_sem, cross_sem, swap_send, swap_recv, out_sem,
):
    me = lax.axis_index("ta")
    g = lax.axis_index("gx")
    odd = lax.rem(me, 2)
    chip = me // 2
    col = lax.rem(chip, COLS)
    line = chip // COLS
    first = me == 0
    last = me == TA - 1
    paired = jnp.logical_not(
        jnp.logical_or(jnp.logical_and(first, g == 0), jnp.logical_and(last, g == GX - 1))
    )
    partner = lax.rem(jnp.where(odd == 0, me + TA - 1, me + 1), TA)
    partner_gx = lax.rem(jnp.where(first, g + GX - 1, jnp.where(last, g + 1, g)), GX)

    gate = pltpu.get_barrier_semaphore()

    def greet(device):
        pl.semaphore_signal(gate, inc=1, device_id=device, device_id_type=MESH)

    def greet_plane(off, carry):
        greet((lax.rem(me + off, TA), g))
        return carry

    lax.fori_loop(1, TA, greet_plane, 0)

    def greet_next(at, carry):
        greet((at, lax.rem(g + 1, GX)))
        return carry

    def greet_previous(at, carry):
        greet((at, lax.rem(g + GX - 1, GX)))
        return carry

    @pl.when(jnp.logical_and(last, g < GX - 1))
    def _():
        lax.fori_loop(0, TA, greet_next, 0)

    @pl.when(jnp.logical_and(first, g > 0))
    def _():
        lax.fori_loop(0, TA, greet_previous, 0)

    pl.semaphore_wait(gate, TA - 1 + jnp.where(g > 0, 1, 0) + jnp.where(g < GX - 1, 1, 0))

    constants = [
        pltpu.make_async_copy(src, dst, const_sem.at[n])
        for n, (src, dst) in enumerate(
            [
                (ion_in, ion_ref),
                (coupling_in, coupling),
                (diffraction_in, diffraction),
                (dft_in, dft),
                (twist_in, twist),
                (within_in, within),
                (before_in, before),
            ]
        )
    ]
    for copy in constants:
        copy.start()

    place = pl.ds(pl.multiple_of(me * 32, 32), 32)

    def send(to, plane, row, slot, count, kind, arrival=None, sem=None):
        pltpu.make_async_remote_copy(
            src_ref=field.at[:, pl.ds(row, count)],
            dst_ref=rx.at[:, pl.ds(slot, count), place],
            send_sem=send_sem.at[kind] if sem is None else sem,
            recv_sem=recv_sem.at[kind if arrival is None else arrival],
            device_id=(to, plane),
            device_id_type=MESH,
        ).start()

    def keep(row, slot, kind):
        pltpu.make_async_copy(
            field.at[:, pl.ds(row, 1)], rx.at[:, pl.ds(slot, 1), place], recv_sem.at[kind]
        ).start()

    def device_at(j, shift, core):
        y = lax.rem(line + j, LINES)
        return 8 * y + 2 * lax.rem(col + shift, COLS) + core

    def send_ahead(j, carry):
        for shift, core in ((3, 0), (1, 1)):
            to = device_at(j, shift, core)

            @pl.when(jnp.logical_and(to > 0, to < TA - 1))
            def _(to=to, core=core):
                send(to, g, 4 * to - 2 + 4 * core, 0, 4, AHEAD)

        return carry

    lax.fori_loop(0, LINES, send_ahead, 0)
    end = 4 * TA - 2
    above, below = lax.rem(g + 1, GX), lax.rem(g + GX - 1, GX)

    @pl.when(col == 1)
    def _():
        send(0, g, 0, 2, 2, AHEAD)

        @pl.when(g < GX - 1)
        def _():
            send(0, above, end, 0, 2, AHEAD)

        @pl.when(g == GX - 1)
        def _():
            send(TA - 1, g, end, 0, 2, AHEAD, FORWARD)

    @pl.when(col == 2)
    def _():
        send(TA - 1, g, end, 0, 2, AHEAD)

        @pl.when(g > 0)
        def _():
            send(TA - 1, below, 0, 2, 2, AHEAD)

        @pl.when(g == 0)
        def _():
            send(0, g, 0, 2, 2, AHEAD, FORWARD)

    for i in range(2):

        def send_inner(off, carry, i=i):
            to = lax.rem(me + off, TA)
            send(to, g, 4 * to + 2 * (1 - lax.rem(to, 2)) + i, 4 + i, 1, INNER + i)
            return carry

        lax.fori_loop(1, TA, send_inner, 0)
        keep(4 * me + 2 * (1 - odd) + i, 4 + i, INNER + i)

    @pl.when(jnp.logical_not(paired))
    def _():
        fe[pl.ds(6 * odd, 2)] = jnp.zeros((2, 2, Y * R, R), F32)

    def arrived(kind, slots, rows):
        ref = rx.at[:, pl.ds(0, slots), pl.ds(0, rows)]
        pltpu.make_async_copy(ref, ref, recv_sem.at[kind]).wait()

    @pl.when(paired)
    def _():
        arrived(AHEAD, 4, 256)

    @pl.when(jnp.logical_not(paired))
    def _():
        arrived(AHEAD, 2, 256)

    def forward(y, slots, rows):
        from_col = lax.rem(col + jnp.where(odd == 0, 1, 3), COLS)
        at = pl.ds(pl.multiple_of(256 * y + 64 * from_col, 64), 64)
        return pltpu.make_async_remote_copy(
            src_ref=rx.at[:, pl.ds(0, 4), at],
            dst_ref=rx.at[:, pl.ds(0, 4), at],
            send_sem=send_sem.at[FORWARD],
            recv_sem=recv_sem.at[FORWARD],
            device_id=(partner, partner_gx),
            device_id_type=MESH,
        )

    @pl.when(paired)
    def _():
        for y in range(LINES):
            forward(y, 4, 256).start()

    direct = ((0, 0), (0, 1), (1, 0), (3, 1))

    def row_of(to, core, kind):
        if kind < NEAR:
            i = kind - OWN
            return (4 * to + i, 2 + i) if core == 0 else (4 * to + 2 + i, i)
        if kind == NEAR:
            return (4 * to - 1, 1) if core == 0 else (4 * to + 4, 2)
        return (4 * to - 2, 0) if core == 0 else (4 * to + 5, 3)

    for kind in (OWN, OWN + 1, NEAR, FAR):

        def send_direct(j, carry, kind=kind):
            for shift, core in direct:
                to = device_at(j, shift, core)
                row, slot = row_of(to, core, kind)
                allowed = to != me
                if kind >= NEAR:
                    allowed = jnp.logical_and(allowed, to != (0 if core == 0 else TA - 1))

                @pl.when(allowed)
                def _(to=to, row=row, slot=slot):
                    send(to, g, row, slot, 1, kind)

            return carry

        lax.fori_loop(0, LINES, send_direct, 0)
        if kind >= NEAR:
            at_end = jnp.logical_or(col == 0, col == 3)
            i = kind - NEAR

            @pl.when(jnp.logical_and(at_end, g < GX - 1))
            def _(kind=kind, i=i):
                send(0, above, end + 1 - i, 1 - i, 1, kind, sem=cross_sem.at[i])

            @pl.when(jnp.logical_and(at_end, g > 0))
            def _(kind=kind, i=i):
                send(TA - 1, below, i, 2 + i, 1, kind, sem=cross_sem.at[2 + i])

        for core in range(2):
            mine = odd == core
            if kind >= NEAR:
                mine = jnp.logical_and(mine, me != (0 if core == 0 else TA - 1))

            @pl.when(mine)
            def _(core=core, kind=kind):
                keep(*row_of(me, core, kind), kind)

    for copy in constants:
        copy.wait()

    def transform(groups):
        real = jnp.concatenate([re for re, _ in groups], axis=1)
        imag = jnp.concatenate([im for _, im in groups], axis=1)
        high, low = halves(jnp.concatenate([real, imag], axis=0))
        table = dft[...]
        section = dot(table, jnp.concatenate([high, high, low], axis=0))
        cos, sin = twist[0], twist[1]
        turned = []
        for n in range(len(groups)):
            re = section[:R, n * R : (n + 1) * R]
            im = section[R:, n * R : (n + 1) * R]
            turned.append(
                jnp.concatenate([re * cos - im * sin, re * sin + im * cos], axis=1)
            )
        high, low = halves(jnp.concatenate(turned, axis=0))
        final = dot_nt(table, jnp.concatenate([high, high, low], axis=1))
        return [
            (final[:R, n * R : (n + 1) * R], final[R:, n * R : (n + 1) * R])
            for n in range(len(groups))
        ]

    def series(slot, y):
        return tuple(rx[c, slot, pl.ds(y, R, stride=Y), :] for c in range(2))

    def plane_of(y):
        return pl.ds(pl.multiple_of(y * R, R), R)

    def own_pair(slot, where, p):
        groups_e, groups_n = [], []
        for side in range(2):
            y = 2 * p + side
            re, im = series(slot, y)
            intensity = re * re + im * im
            rate = ion_ref[y, 4 * me + where - 2] * jnp.exp(
                -BARRIER * lax.rsqrt(intensity + 1.0)
            )
            sums = dot(jnp.concatenate(halves(rate), axis=1), within[...])
            earlier = dot(before[...], jnp.concatenate(halves(sums[:, R:]), axis=0))
            plasma = 1.0 - jnp.exp(-(sums[:, :R] + earlier))
            groups_e.append((re, im))
            kerr = KERR * intensity
            groups_n.append((-kerr * im - plasma * re, kerr * re - plasma * im))
        spectra = transform(groups_e + groups_n)
        c = coupling[...]
        for side in range(2):
            at = plane_of(2 * p + side)
            e_re, e_im = spectra[side]
            n_re, n_im = spectra[2 + side]
            fe[where, 0, at, :] = e_re
            fe[where, 1, at, :] = e_im
            part[where - 2, 0, at, :] = e_re - c * n_im
            part[where - 2, 1, at, :] = e_im + c * n_re

    def halo_four(slot, where, p):
        spectra = transform([series(slot, 4 * p + side) for side in range(4)])
        for side in range(4):
            at = plane_of(4 * p + side)
            fe[where, 0, at, :], fe[where, 1, at, :] = spectra[side]

    def swap(i):
        where = 4 + i - 2 * odd
        return pltpu.make_async_remote_copy(
            src_ref=fe.at[where],
            dst_ref=fe.at[jnp.where(odd == 0, i, 6 + i)],
            send_sem=swap_send.at[i],
            recv_sem=swap_recv.at[i],
            device_id=(me + 1 - 2 * odd, g),
            device_id_type=MESH,
        )

    def own_row(step, carry):
        for i in range(2):

            @pl.when(step == i)
            def _(i=i):
                arrived(INNER + i, 1, 1024)

            @pl.when(step == 2 + i)
            def _(i=i):
                arrived(OWN + i, 1, 512)

        @pl.when(jnp.logical_and(step == 2, paired))
        def _():
            arrived(FORWARD, 4, 256)

        @pl.when(jnp.logical_and(step == 2, jnp.logical_not(paired)))
        def _():
            arrived(FORWARD, 2, 256)

        slot = jnp.where(step < 2, 4 + step, step - 2 * odd)
        where = jnp.where(step < 2, 4 + step - 2 * odd, step + 2 * odd)

        def body(p, carry):
            own_pair(slot, where, p)
            return carry

        lax.fori_loop(0, Y // 2, body, 0)
        for i in range(2):

            @pl.when(step == i)
            def _(i=i):
                swap(i).start()

        return carry

    lax.fori_loop(0, ROWS, own_row, 0)

    def finish(row):
        def block(n, carry):
            k = pl.multiple_of(n * 8, 8)
            d = diffraction[pl.ds(k, 8), :] * (1.0 / 12.0)
            lap = []
            for c in range(2):
                mid = [fe[row + 2, c, pl.ds(y * R + k, 8), :] for y in range(Y)]
                planes = []
                for y in range(Y):
                    at = pl.ds(y * R + k, 8)
                    near = fe[row + 1, c, at, :] + fe[row + 3, c, at, :]
                    far = fe[row, c, at, :] + fe[row + 4, c, at, :]
                    for o in (-1, 1):
                        if 0 <= y + o < Y:
                            near = near + mid[y + o]
                    for o in (-2, 2):
                        if 0 <= y + o < Y:
                            far = far + mid[y + o]
                    planes.append(16.0 * near - far - 60.0 * mid[y])
                lap.append(planes)
            for y in range(Y):
                at = pl.ds(y * R + k, 8)
                to = pl.ds(k * Y + y, 8, stride=Y)
                result[row, 0, to, :] = part[row, 0, at, :] - d * lap[1][y]
                result[row, 1, to, :] = part[row, 1, at, :] + d * lap[0][y]
            return carry

        lax.fori_loop(0, R // 8, block, 0)
        pltpu.make_async_copy(result.at[row], out.at[:, row], out_sem.at[row]).start()

    for i in range(2):
        swap(i).wait()

    def finish_inner(n, carry):
        finish(jnp.where(odd == 0, 3 - n, n))
        return carry

    lax.fori_loop(0, 2, finish_inner, 0)

    def finish_outer(n, carry):
        @pl.when(paired)
        def _():
            for i in range(2):

                @pl.when(n == i)
                def _(i=i):
                    arrived(NEAR + i, 1, 512)

            slot = jnp.where(odd == 0, 1 - n, 2 + n)

            def body(p, carry):
                halo_four(slot, slot + 4 * odd, p)
                return carry

            lax.fori_loop(0, Y // 4, body, 0)

        finish(jnp.where(odd == 0, 1 - n, 2 + n))
        return carry

    lax.fori_loop(0, 2, finish_outer, 0)

    def sent(kind, slots, rows):
        ref = rx.at[:, pl.ds(0, slots), pl.ds(0, rows)]
        pltpu.make_async_copy(ref, ref, send_sem.at[kind]).wait()

    sent(AHEAD, 4, 256)

    @pl.when(paired)
    def _():
        sent(FORWARD, 4, 256)

    for i in range(2):
        sent(INNER + i, 1, 31 * 32)
        sent(OWN + i, 1, 15 * 32)
        at_end = jnp.logical_or(col == 0, col == 3)
        tip = jnp.logical_or(first, last)

        @pl.when(jnp.logical_not(at_end))
        def _(i=i):
            sent(NEAR + i, 1, 15 * 32)

        @pl.when(tip)
        def _(i=i):
            sent(NEAR + i, 1, 14 * 32)

        @pl.when(jnp.logical_and(at_end, jnp.logical_not(tip)))
        def _(i=i):
            sent(NEAR + i, 1, 13 * 32)

        for n, there in enumerate((g < GX - 1, g > 0)):

            @pl.when(jnp.logical_and(at_end, there))
            def _(i=i, n=n):
                ref = rx.at[:, pl.ds(0, 1), pl.ds(0, 32)]
                pltpu.make_async_copy(ref, ref, cross_sem.at[2 * n + i]).wait()

    for row in range(ROWS):
        pltpu.make_async_copy(result.at[row], out.at[:, row], out_sem.at[row]).wait()


def on_device(field, ion_rate, diffraction, coupling):
    x_rows = field.shape[1]
    tiles = field.reshape(2, x_rows, Y, 4, R).transpose(0, 1, 3, 2, 4).reshape(2, x_rows, 32, R)
    dft, twist, within, before = tables()
    hbm = pl.BlockSpec(memory_space=pl.ANY)
    spectrum = pl.pallas_call(
        kernel,
        out_shape=jax.ShapeDtypeStruct((2, ROWS, R * Y, R), F32),
        in_specs=[hbm] * 8,
        out_specs=hbm,
        scratch_shapes=[
            pltpu.VMEM((2, ROWS + 2, R * Y, R), F32),
            pltpu.VMEM((ROWS + 4, 2, Y * R, R), F32),
            pltpu.VMEM((ROWS, 2, Y * R, R), F32),
            pltpu.VMEM((ROWS, 2, R * Y, R), F32),
            pltpu.SMEM((Y, x_rows), F32),
            pltpu.VMEM((R, R), F32),
            pltpu.VMEM((R, R), F32),
            pltpu.VMEM(dft.shape, BF16),
            pltpu.VMEM(twist.shape, F32),
            pltpu.VMEM(within.shape, BF16),
            pltpu.VMEM(before.shape, BF16),
            pltpu.SemaphoreType.DMA((7,)),
            pltpu.SemaphoreType.DMA((8,)),
            pltpu.SemaphoreType.DMA((8,)),
            pltpu.SemaphoreType.DMA((4,)),
            pltpu.SemaphoreType.DMA((2,)),
            pltpu.SemaphoreType.DMA((2,)),
            pltpu.SemaphoreType.DMA((ROWS,)),
        ],
        compiler_params=pltpu.CompilerParams(
            collective_id=0, has_side_effects=True, vmem_limit_bytes=60 * 1024 * 1024
        ),
    )(
        ion_rate.T,
        tiles,
        coupling.reshape(R, R),
        diffraction.reshape(R, R),
        jnp.asarray(dft),
        jnp.asarray(twist),
        jnp.asarray(within),
        jnp.asarray(before),
    )
    spectrum = spectrum.reshape(2, ROWS, R, Y, R).transpose(0, 1, 3, 2, 4)
    return spectrum.reshape(2, ROWS, Y, R * R)


def solution(mesh):
    in_specs = (P(None, "gx", None, "ta"), P("gx", None), P(), P())
    out_specs = P(None, ("gx", "ta"), None, None)
    return jax.shard_map(
        on_device, mesh=mesh, in_specs=in_specs, out_specs=out_specs, check_vma=False
    )
```

time: 94.3 us -> 99.7 us (1.057)
  the two profiles are of different devices: /device:TPU:96 before, /device:TPU:1 now
where the time goes in v2:
time: 99.7 us; the launch traced here: 99.6 us
  Pallas kernels  95.1 us (95%)
  local copies, waits for them, and re-layouts  4.5 us (5%)
    pallas_call x1, Pallas kernels, on_device(): pl.pallas_call(kernel, out_shape=jax.ShapeDtypeStruct((2, ROWS, R * Y, R)...  95.1 us
    unnamed x1, local copies, waits for them, and re-layouts  4.5 us

profile of v2, /device:TPU:1, one launch (start us, length us, event | category | flops | bytes accessed | tf_op | source)
XLA Modules:
  0.0 99.6 jit_solution(4904680255392068150)
XLA Ops:
  0.0 95.1 %shard_map.82 = f32[2,4,1024,128]{3,2,1,0:T(8,128)} custom-call(f32[8,128]{1,0:T(8,128)} %bitcast.17, f32[2,128,32,128]{3,2,1,0:T(8,128)} %bitcast.14, f32[128,128]{1,0:T(8,128)} %bitcast.15, f32[128,128]{1,0:T(8,128)} %bitcast.16, bf16[256,768]{1,0:T(8,128)(2,1)} %constant.8.clone.dft_in, f32[2,128,128]{2,1,0:T(8,128)} %constant.9.clone.twist_in, ...), custom_call_target="tpu_custom_call" | custom-call | tf_op jit(solution)/shard_map/pallas_call | solution.py:494
  95.1 4.5 %copy.10 = f32[2,4,8,16384]{3,2,1,0:T(8,128)} copy(f32[2,4,8,16384]{3,2,1,0:T(8,128)} %bitcast.13) | data formatting | bytes 8388608

commit v3 on v1

--- a/solution.py
+++ b/solution.py
@@ -17,6 +17,7 @@
 GX = 4
 ROWS = 4
 Y = 8
+PIECES = 4
 F32 = jnp.float32
 BF16 = jnp.bfloat16
 
@@ -58,10 +59,10 @@
 
 
 def kernel(
-    ion_ref, field, coupling_in, diffraction_in, dft_in, twist_in, within_in, before_in,
-    out,
-    rx, fe, part, result, coupling, diffraction, dft, twist, within, before,
-    const_sem, send_sem, recv_sem, halo_send, halo_recv, out_sem,
+    ion_in, field, coupling_in, diffraction_in, dft_in, twist_in, within_in, before_in,
+    q_out, halo_out,
+    rx, fe, part, result, blank, ion_ref, coupling, diffraction, dft, twist, within, before,
+    const_sem, send_sem, recv_sem, halo_send, halo_recv, blank_sem, out_sem,
 ):
     me = lax.axis_index("ta")
     g = lax.axis_index("gx")
@@ -93,6 +94,7 @@
         pltpu.make_async_copy(src, dst, const_sem.at[n])
         for n, (src, dst) in enumerate(
             [
+                (ion_in, ion_ref),
                 (coupling_in, coupling),
                 (diffraction_in, diffraction),
                 (dft_in, dft),
@@ -106,42 +108,73 @@
         copy.start()
 
     place = pl.ds(pl.multiple_of(me * 32, 32), 32)
+    def send(to, step):
+        row = row_at(step, lax.rem(to, 2))
+        pltpu.make_async_remote_copy(
+            src_ref=field.at[:, 4 * to + row],
+            dst_ref=rx.at[row, :, place],
+            send_sem=send_sem.at[step],
+            recv_sem=recv_sem.at[step],
+            device_id=(to, g),
+            device_id_type=MESH,
+        ).start()
+
+    def send_ends(j, carry):
+        for at in (0, 7):
+            to = 8 * lax.rem(me // 8 + j, 4) + at
+
+            @pl.when(to != me)
+            def _(to=to):
+                send(to, 0)
+                send(to, 1)
+
+        return carry
+
+    lax.fori_loop(0, 4, send_ends, 0)
+
     for step in range(ROWS):
 
-        def send(off, carry, step=step):
+        def send_row(off, carry, step=step):
             to = lax.rem(me + off, TA)
-            row = row_at(step, lax.rem(to, 2))
-            pltpu.make_async_remote_copy(
-                src_ref=field.at[:, 4 * to + row],
-                dst_ref=rx.at[row, :, place],
-                send_sem=send_sem.at[step],
-                recv_sem=recv_sem.at[step],
-                device_id=(to, g),
-                device_id_type=MESH,
-            ).start()
+            if step < 2:
+                at = lax.rem(to, 8)
+
+                @pl.when(jnp.logical_and(at > 0, at < 7))
+                def _():
+                    send(to, step)
+
+            else:
+                send(to, step)
             return carry
 
-        lax.fori_loop(1, TA, send, 0)
+        lax.fori_loop(1, TA, send_row, 0)
         own = row_at(step, odd)
         pltpu.make_async_copy(
             field.at[:, 4 * me + own], rx.at[own, :, place], recv_sem.at[step]
         ).start()
 
+    def blank_copy(slot):
+        return pltpu.make_async_copy(blank, halo_out.at[slot], blank_sem.at[slot])
+
     @pl.when(jnp.logical_not(has_left))
     def _():
-        fe[0:2] = jnp.zeros((2, 2, Y * R, R), F32)
+        blank[...] = jnp.zeros_like(blank)
+        blank_copy(0).start()
+        blank_copy(1).start()
 
     @pl.when(jnp.logical_not(has_right))
     def _():
-        fe[6:8] = jnp.zeros((2, 2, Y * R, R), F32)
+        blank[...] = jnp.zeros_like(blank)
+        blank_copy(2).start()
+        blank_copy(3).start()
 
     for copy in constants:
         copy.wait()
 
     def halo_copy(row, to_left):
         return pltpu.make_async_remote_copy(
-            src_ref=fe.at[row + 2],
-            dst_ref=fe.at[lax.rem(row + 6, 8)],
+            src_ref=fe.at[row],
+            dst_ref=halo_out.at[lax.rem(row + 2, ROWS)],
             send_sem=halo_send.at[row],
             recv_sem=halo_recv.at[row],
             device_id=(left_ta, left_gx) if to_left else (right_ta, right_gx),
@@ -176,7 +209,7 @@
             re = rx[row, 0, pl.ds(y, R, stride=Y), :]
             im = rx[row, 1, pl.ds(y, R, stride=Y), :]
             intensity = re * re + im * im
-            rate = ion_ref[4 * me + row, y] * jnp.exp(-BARRIER * lax.rsqrt(intensity + 1.0))
+            rate = ion_ref[y, 4 * me + row] * jnp.exp(-BARRIER * lax.rsqrt(intensity + 1.0))
             sums = dot(jnp.concatenate(halves(rate), axis=1), within[...])
             earlier = dot(before[...], jnp.concatenate(halves(sums[:, R:]), axis=0))
             plasma = 1.0 - jnp.exp(-(sums[:, :R] + earlier))
@@ -189,65 +222,48 @@
             at = pl.ds(pl.multiple_of((2 * p + side) * R, R), R)
             e_re, e_im = spectra[side]
             n_re, n_im = spectra[2 + side]
-            fe[row + 2, 0, at, :] = e_re
-            fe[row + 2, 1, at, :] = e_im
+            fe[row, 0, at, :] = e_re
+            fe[row, 1, at, :] = e_im
             part[row, 0, at, :] = e_re - c * n_im
             part[row, 1, at, :] = e_im + c * n_re
 
-    for step in range(ROWS):
+    def own_row(step, carry):
         row = row_at(step, odd)
         pltpu.make_async_copy(rx.at[row], rx.at[row], recv_sem.at[step]).wait()
 
-        def body(p, carry, row=row):
+        def body(p, carry):
             pair(row, p)
             return carry
 
-        lax.fori_loop(0, Y // 2, body, 0)
+        lax.fori_loop(0, Y // 2, body, 0, unroll=4)
 
         @pl.when(jnp.logical_and(row < 2, has_left))
-        def _(row=row):
+        def _():
             halo_copy(row, True).start()
 
         @pl.when(jnp.logical_and(row >= 2, has_right))
-        def _(row=row):
+        def _():
             halo_copy(row, False).start()
 
-    def arrived(row):
-        pltpu.make_async_copy(
-            fe.at[lax.rem(row + 6, 8)], fe.at[lax.rem(row + 6, 8)], halo_recv.at[row]
-        ).wait()
-
-    def left_arrived():
-        @pl.when(has_left)
-        def _():
-            arrived(2)
-            arrived(3)
-
-    def right_arrived():
-        @pl.when(has_right)
-        def _():
-            arrived(0)
-            arrived(1)
-
-    def finish(row):
+        return carry
+
+    lax.fori_loop(0, ROWS, own_row, 0)
+
+    def inner_terms(row):
         def block(n, carry):
             k = pl.multiple_of(n * 8, 8)
             d = diffraction[pl.ds(k, 8), :] * (1.0 / 12.0)
             lap = []
             for c in range(2):
-                mid = [fe[row + 2, c, pl.ds(y * R + k, 8), :] for y in range(Y)]
+                mid = [fe[row, c, pl.ds(y * R + k, 8), :] for y in range(Y)]
                 planes = []
                 for y in range(Y):
                     at = pl.ds(y * R + k, 8)
-                    near = fe[row + 1, c, at, :] + fe[row + 3, c, at, :]
-                    far = fe[row, c, at, :] + fe[row + 4, c, at, :]
-                    for o in (-1, 1):
-                        if 0 <= y + o < Y:
-                            near = near + mid[y + o]
-                    for o in (-2, 2):
-                        if 0 <= y + o < Y:
-                            far = far + mid[y + o]
-                    planes.append(16.0 * near - far - 60.0 * mid[y])
+                    near = [fe[row + o, c, at, :] for o in (-1, 1) if 0 <= row + o < ROWS]
+                    near += [mid[y + o] for o in (-1, 1) if 0 <= y + o < Y]
+                    far = [fe[row + o, c, at, :] for o in (-2, 2) if 0 <= row + o < ROWS]
+                    far += [mid[y + o] for o in (-2, 2) if 0 <= y + o < Y]
+                    planes.append(16.0 * sum(near[1:], near[0]) - sum(far[1:], far[0]) - 60.0 * mid[y])
                 lap.append(planes)
             for y in range(Y):
                 at = pl.ds(y * R + k, 8)
@@ -257,33 +273,13 @@
             return carry
 
         lax.fori_loop(0, R // 8, block, 0)
-        copy = pltpu.make_async_copy(result.at[row], out.at[:, row], out_sem.at[row])
-        copy.start()
-
-    @pl.when(odd == 0)
-    def _():
-        left_arrived()
-
-    @pl.when(odd == 1)
-    def _():
-        right_arrived()
-
-    for step in range(2):
-        finish(row_at(step, odd))
-
-    @pl.when(odd == 0)
-    def _():
-        right_arrived()
-
-    @pl.when(odd == 1)
-    def _():
-        left_arrived()
-
-    for step in range(2, ROWS):
-        finish(row_at(step, odd))
+        pltpu.make_async_copy(result.at[row], q_out.at[:, row], out_sem.at[row]).start()
 
     for row in range(ROWS):
-        pltpu.make_async_copy(result.at[row], out.at[:, row], out_sem.at[row]).wait()
+        inner_terms(row)
+
+    for row in range(ROWS):
+        pltpu.make_async_copy(result.at[row], q_out.at[:, row], out_sem.at[row]).wait()
     for step in range(ROWS):
         sent = rx.at[0, :, pl.ds(0, (TA - 1) * 32)]
         pltpu.make_async_copy(sent, sent, send_sem.at[step]).wait()
@@ -292,6 +288,66 @@
         @pl.when(has_left if row < 2 else has_right)
         def _(row=row):
             halo_copy(row, row < 2).wait_send()
+
+    for row in range(ROWS):
+        slot = (row + 2) % ROWS
+        there = has_right if row < 2 else has_left
+
+        @pl.when(there)
+        def _(row=row, slot=slot):
+            pltpu.make_async_copy(halo_out.at[slot], halo_out.at[slot], halo_recv.at[row]).wait()
+
+        @pl.when(jnp.logical_not(there))
+        def _(slot=slot):
+            blank_copy(slot).wait()
+
+
+def add_halo(
+    q_in, halo_in, diffraction_in, out,
+    q, halo, diffraction, result, q_sem, halo_sem, d_sem, out_sem,
+):
+    depth = R // PIECES
+
+    def copies(n):
+        wide = pl.ds(n * depth * Y, depth * Y)
+        thin = pl.ds(n * depth, depth)
+        return (
+            pltpu.make_async_copy(q_in.at[:, :, wide], q.at[:, :, wide], q_sem.at[n]),
+            pltpu.make_async_copy(
+                halo_in.at[:, :, :, thin], halo.at[:, :, :, thin], halo_sem.at[n]
+            ),
+            pltpu.make_async_copy(result.at[:, :, wide], out.at[:, :, wide], out_sem.at[n]),
+        )
+
+    first = pltpu.make_async_copy(diffraction_in, diffraction, d_sem)
+    first.start()
+    for n in range(PIECES):
+        for copy in copies(n)[:2]:
+            copy.start()
+    first.wait()
+    for n in range(PIECES):
+        for copy in copies(n)[:2]:
+            copy.wait()
+
+        def block(i, carry, n=n):
+            k = pl.multiple_of(n * depth + 8 * i, 8)
+            at_k = pl.ds(k, 8)
+            d = diffraction[at_k, :] * (1.0 / 12.0)
+            for y in range(Y):
+                lap = []
+                for c in range(2):
+                    h = [halo[slot, c, y, at_k, :] for slot in range(4)]
+                    lap.append((16.0 * h[1] - h[0], -h[1], -h[2], 16.0 * h[2] - h[3]))
+                at = pl.ds(k * Y + y, 8, stride=Y)
+                for row in range(ROWS):
+                    result[0, row, at, :] = q[0, row, at, :] - d * lap[1][row]
+                    result[1, row, at, :] = q[1, row, at, :] + d * lap[0][row]
+            return carry
+
+        lax.fori_loop(0, depth // 8, block, 0)
+        copies(n)[2].start()
+    for n in range(PIECES):
+        copies(n)[2].wait()
 
 
 def on_device(field, ion_rate, diffraction, coupling):
@@ -299,23 +355,29 @@
     tiles = field.reshape(2, x_rows, Y, 4, R).transpose(0, 1, 3, 2, 4).reshape(2, x_rows, 32, R)
     dft, twist, within, before = tables()
     hbm = pl.BlockSpec(memory_space=pl.ANY)
-    spectrum = pl.pallas_call(
+    q, halo = pl.pallas_call(
         kernel,
-        out_shape=jax.ShapeDtypeStruct((2, ROWS, R * Y, R), F32),
-        in_specs=[pl.BlockSpec(memory_space=pltpu.SMEM)] + [hbm] * 7,
-        out_specs=hbm,
+        out_shape=[
+            jax.ShapeDtypeStruct((2, ROWS, R * Y, R), F32),
+            jax.ShapeDtypeStruct((4, 2, Y * R, R), F32),
+        ],
+        in_specs=[hbm] * 8,
+        out_specs=[hbm, hbm],
         scratch_shapes=[
             pltpu.VMEM((ROWS, 2, R * Y, R), F32),
-            pltpu.VMEM((ROWS + 4, 2, Y * R, R), F32),
+            pltpu.VMEM((ROWS, 2, Y * R, R), F32),
             pltpu.VMEM((ROWS, 2, Y * R, R), F32),
             pltpu.VMEM((ROWS, 2, R * Y, R), F32),
+            pltpu.VMEM((2, Y * R, R), F32),
+            pltpu.SMEM((Y, x_rows), F32),
             pltpu.VMEM((R, R), F32),
             pltpu.VMEM((R, R), F32),
             pltpu.VMEM(dft.shape, BF16),
             pltpu.VMEM(twist.shape, F32),
             pltpu.VMEM(within.shape, BF16),
             pltpu.VMEM(before.shape, BF16),
-            pltpu.SemaphoreType.DMA((6,)),
+            pltpu.SemaphoreType.DMA((7,)),
+            pltpu.SemaphoreType.DMA((ROWS,)),
             pltpu.SemaphoreType.DMA((ROWS,)),
             pltpu.SemaphoreType.DMA((ROWS,)),
             pltpu.SemaphoreType.DMA((ROWS,)),
@@ -323,10 +385,10 @@
             pltpu.SemaphoreType.DMA((ROWS,)),
         ],
         compiler_params=pltpu.CompilerParams(
-            collective_id=0, has_side_effects=True, vmem_limit_bytes=48 * 1024 * 1024
+            collective_id=0, has_side_effects=True, vmem_limit_bytes=60 * 1024 * 1024
         ),
     )(
-        ion_rate,
+        ion_rate.T,
         tiles,
         coupling.reshape(R, R),
         diffraction.reshape(R, R),
@@ -335,6 +397,23 @@
         jnp.asarray(within),
         jnp.asarray(before),
     )
+    spectrum = pl.pallas_call(
+        add_halo,
+        out_shape=jax.ShapeDtypeStruct((2, ROWS, R * Y, R), F32),
+        in_specs=[hbm] * 3,
+        out_specs=hbm,
+        scratch_shapes=[
+            pltpu.VMEM((2, ROWS, R * Y, R), F32),
+            pltpu.VMEM((4, 2, Y, R, R), F32),
+            pltpu.VMEM((R, R), F32),
+            pltpu.VMEM((2, ROWS, R * Y, R), F32),
+            pltpu.SemaphoreType.DMA((PIECES,)),
+            pltpu.SemaphoreType.DMA((PIECES,)),
+            pltpu.SemaphoreType.DMA,
+            pltpu.SemaphoreType.DMA((PIECES,)),
+        ],
+        compiler_params=pltpu.CompilerParams(vmem_limit_bytes=60 * 1024 * 1024),
+    )(q, halo.reshape(4, 2, Y, R, R), diffraction.reshape(R, R))
     spectrum = spectrum.reshape(2, ROWS, R, Y, R).transpose(0, 1, 3, 2, 4)
     return spectrum.reshape(2, ROWS, Y, R * R)
 

time: 94.3 us -> 84.8 us (0.90)
  local copies, waits for them, and re-layouts: 8.12 us -> 0 us
    unnamed x14 -> x0, local copies, waits for them, and re-layouts: 8.12 us -> none
    pallas_call x1 -> x2, Pallas kernels: 85.4 us -> 84.7 us  [the longest x1 79.3 us: on_device(): pl.pallas_call(kernel, out_shape=[jax.ShapeDtypeStruct((2, ROWS, R * Y, R...]
where the time goes in v3:
time: 84.8 us; the launch traced here: 84.7 us
  Pallas kernels  84.7 us (100%)
    pallas_call x1, Pallas kernels, on_device(): pl.pallas_call(kernel, out_shape=[jax.ShapeDtypeStruct((2, ROWS, R * Y, R...  79.3 us
    pallas_call x1, Pallas kernels, on_device(): pl.pallas_call(add_halo, out_shape=jax.ShapeDtypeStruct((2, ROWS, R * Y,...  5.41 us

profile of v3, /device:TPU:96, one launch (start us, length us, event | category | flops | bytes accessed | tf_op | source)
XLA Modules:
  0.0 84.7 jit_solution(7364202108357997115)
XLA Ops:
  0.0 79.3 %shard_map.82 = (f32[2,4,1024,128]{3,2,1,0:T(8,128)}, f32[4,2,1024,128]{3,2,1,0:T(8,128)}) custom-call(f32[8,128]{1,0:T(8,128)} %bitcast.19, f32[2,128,32,128]{3,2,1,0:T(8,128)} %bitcast.15, f32[128,128]{1,0:T(8,128)} %bitcast.18, f32[128,128]{1,0:T(8,128)} %bitcast.16, bf16[256,768]{1,0:T(8,128)(2,1)} %constant.8.clone.dft_in, ...), custom_call_target="tpu_custom_call" | custom-call | tf_op jit(solution)/shard_map/pallas_call | solution.py:358
  79.3 5.4 %shard_map.83 = f32[2,4,1024,128]{3,2,1,0:T(8,128)} custom-call(f32[2,4,1024,128]{3,2,1,0:T(8,128)} %get-tuple-element.7.q_in, f32[4,2,8,128,128]{4,3,2,1,0:T(8,128)} %bitcast.14, f32[128,128]{1,0:T(8,128)} %bitcast.17), custom_call_target="tpu_custom_call" | custom-call | tf_op jit(solution)/shard_map/pallas_call | solution.py:400

commit v4 on v3

v4 whole, which is shorter than its diff:
```python
import functools
import math

import jax
import jax.numpy as jnp
import ml_dtypes
import numpy as np
from jax import lax
from jax.experimental import pallas as pl
from jax.experimental.pallas import tpu as pltpu
from jax.sharding import PartitionSpec as P

BARRIER = 2.0
KERR = 0.5
MESH = pl.DeviceIdType.MESH
R = 128
TA = 32
GX = 4
ROWS = 4
Y = 8
LINES = 4
COLS = 4
INNER, THEIRS, OWN, AHEAD, NEAR, FAR = 0, 2, 3, 4, 5, 6
BOUNDARY_STEP = 1
FORWARD_STEP = 2
DETOUR = (2,)
COPY_AFTER = 1
PIECES = 4
F32 = jnp.float32
BF16 = jnp.bfloat16


def tables():
    index = np.arange(R)
    angle = 2.0 * np.pi / R * (np.outer(index, index) % R)
    cos, sin = np.cos(angle), np.sin(angle)
    full = np.block([[cos, sin], [-sin, cos]]).astype(np.float32)
    high = full.astype(ml_dtypes.bfloat16)
    low = (full - high.astype(np.float32)).astype(ml_dtypes.bfloat16)
    dft = np.concatenate([high, low, high], axis=1)
    turn = 2.0 * np.pi / (R * R) * np.outer(index, index)
    twist = np.stack([np.cos(turn), -np.sin(turn)]) / R
    upper = (index[:, None] <= index[None, :]).astype(np.float32)
    within = np.concatenate([upper, np.ones((R, R), np.float32)], axis=1)
    within = np.concatenate([within, within], axis=0)
    lower = (index[:, None] > index[None, :]).astype(np.float32)
    before = np.concatenate([lower, lower], axis=1)
    return (
        dft,
        twist.astype(np.float32),
        within.astype(ml_dtypes.bfloat16),
        before.astype(ml_dtypes.bfloat16),
    )


def detours(lines):
    return functools.reduce(jnp.logical_or, [lines == n for n in DETOUR])


def halves(v):
    high = v.astype(BF16)
    return high, (v - high.astype(F32)).astype(BF16)


def dot(a, b):
    return jnp.dot(a, b, preferred_element_type=F32)


def dot_nt(a, b):
    return lax.dot_general(a, b, (((1,), (1,)), ((), ())), preferred_element_type=F32)


def kernel(
    ion_in, field, coupling_in, diffraction_in, dft_in, twist_in, within_in, before_in,
    q_out, halo_out,
    rx, fe, part, result, side, ion_ref, coupling, diffraction, dft, twist, within, before,
    const_sem, send_sem, recv_sem, swap_send, swap_recv, halo_send, halo_recv, side_sem, out_sem,
):
    me = lax.axis_index("ta")
    g = lax.axis_index("gx")
    odd = lax.rem(me, 2)
    away = 1 - 2 * odd
    chip = me // 2
    col = lax.rem(chip, COLS)
    line = chip // COLS
    first, last = me == 0, me == TA - 1
    at_end = jnp.logical_or(lax.rem(me, 8) == 0, lax.rem(me, 8) == 7)
    plain = jnp.logical_not(at_end)
    tip = jnp.logical_or(jnp.logical_and(first, g == 0), jnp.logical_and(last, g == GX - 1))
    paired = jnp.logical_not(tip)
    cross = jnp.logical_and(paired, jnp.logical_or(first, last))
    spectral = jnp.logical_and(paired, at_end)
    wide = jnp.logical_or(
        jnp.logical_and(odd == 0, col == 1), jnp.logical_and(odd == 1, col == COLS - 2)
    )
    thin = jnp.logical_or(
        jnp.logical_and(odd == 1, col == 0), jnp.logical_and(odd == 0, col == COLS - 1)
    )
    even_share = jnp.logical_and(plain, jnp.logical_not(jnp.logical_or(wide, thin)))
    partner = lax.rem(me + TA - away, TA)
    partner_gx = jnp.where(first, lax.rem(g + GX - 1, GX), jnp.where(last, lax.rem(g + 1, GX), g))

    gate = pltpu.get_barrier_semaphore()

    def greet(off, carry):
        pl.semaphore_signal(
            gate, inc=1, device_id=(lax.rem(me + off, TA), g), device_id_type=MESH
        )
        return carry

    lax.fori_loop(1, TA, greet, 0)

    @pl.when(cross)
    def _():
        pl.semaphore_signal(gate, inc=1, device_id=(partner, partner_gx), device_id_type=MESH)

    pl.semaphore_wait(gate, TA - 1 + jnp.where(cross, 1, 0))

    constants = [
        pltpu.make_async_copy(src, dst, const_sem.at[n])
        for n, (src, dst) in enumerate(
            [
                (ion_in, ion_ref),
                (coupling_in, coupling),
                (diffraction_in, diffraction),
                (dft_in, dft),
                (twist_in, twist),
                (within_in, within),
                (before_in, before),
            ]
        )
    ]
    for copy in constants:
        copy.start()

    place = pl.ds(pl.multiple_of(me * 32, 32), 32)

    def send(to, row, slot, count, kind):
        pltpu.make_async_remote_copy(
            src_ref=field.at[:, pl.ds(row, count)],
            dst_ref=rx.at[:, pl.ds(slot, count), place],
            send_sem=send_sem.at[kind],
            recv_sem=recv_sem.at[kind],
            device_id=(to, g),
            device_id_type=MESH,
        ).start()

    def keep(row, slot, count, kind):
        pltpu.make_async_copy(
            field.at[:, pl.ds(row, count)],
            rx.at[:, pl.ds(slot, count), place],
            recv_sem.at[kind],
        ).start()

    def deliver(act, core, kind, to):
        if kind == OWN:
            act(4 * to + 2 * core, 2 - 2 * core, 2, OWN)
        else:
            act(4 * to - 2 + 6 * core, 2 * core, 2, THEIRS)

    def boundary_sends(kind):
        def at_line(j, carry):
            y = lax.rem(line + j, LINES)
            detour = detours(lax.rem(LINES - j, LINES))
            for shift, core in ((2, 0), (2, 1), (3, 0), (1, 1), (0, 0), (0, 1)):
                column = lax.rem(col + shift, COLS)
                to = 8 * y + 2 * column + core
                fits = column != (0 if core == 0 else COLS - 1)
                if shift == 2:
                    fits = jnp.logical_and(col == (COLS - 1 if core == 0 else 0), detour)
                if shift in (1, 3):
                    far = column == (COLS - 1 if core == 0 else 0)
                    fits = jnp.logical_and(fits, jnp.logical_not(jnp.logical_and(far, detour)))
                if shift == 0:
                    fits = jnp.logical_and(fits, to != me)

                @pl.when(fits)
                def _(to=to, core=core):
                    deliver(functools.partial(send, to), core, kind, to)

            return carry

        lax.fori_loop(0, LINES, at_line, 0)
        for core in range(2):

            @pl.when(jnp.logical_and(plain, odd == core))
            def _(core=core):
                deliver(keep, core, kind, me)

    def end_sends():
        def at_line(j, carry):
            y = lax.rem(line + j, LINES)
            for to, core in ((8 * y, 0), (8 * y + 7, 1)):

                @pl.when(to != me)
                def _(to=to, core=core):
                    deliver(functools.partial(send, to), core, OWN, to)

            return carry

        lax.fori_loop(0, LINES, at_line, 0)
        for core in range(2):

            @pl.when(jnp.logical_and(at_end, odd == core))
            def _(core=core):
                deliver(keep, core, OWN, me)

    def inner_sends(i):
        def send_inner(off, carry):
            to = lax.rem(me + off, TA)
            send(to, 4 * to + 2 * (1 - lax.rem(to, 2)) + i, 4 + i, 1, INNER + i)
            return carry

        lax.fori_loop(1, TA, send_inner, 0)
        keep(4 * me + 2 * (1 - odd) + i, 4 + i, 1, INNER + i)

    def wait_for(sem, slots, rows):
        ref = rx.at[:, pl.ds(0, slots), pl.ds(0, rows)]
        pltpu.make_async_copy(ref, ref, sem).wait()

    def share(action, of_partner=False):
        more, less = 512 + 64 * len(DETOUR), 512 - 64 * len(DETOUR)
        for when, rows in (
            (even_share, 512),
            (thin if of_partner else wide, more),
            (wide if of_partner else thin, less),
        ):

            @pl.when(when)
            def _(rows=rows):
                action(rows)

    def forward(slot, count, kind):
        def one(column, y):
            at = pl.ds(pl.multiple_of(256 * y + 64 * column, 64), 64)
            pltpu.make_async_remote_copy(
                src_ref=rx.at[:, pl.ds(slot, count), at],
                dst_ref=rx.at[:, pl.ds(slot, count), at],
                send_sem=send_sem.at[kind],
                recv_sem=recv_sem.at[kind],
                device_id=(partner, partner_gx),
                device_id_type=MESH,
            ).start()

        def at_line(y, carry):
            detour = detours(lax.rem(y - line + LINES, LINES))
            one(col, y)

            @pl.when(jnp.logical_not(jnp.logical_and(thin, detour)))
            def _():
                one(lax.rem(col + jnp.where(odd == 0, 1, 3), COLS), y)

            @pl.when(jnp.logical_and(wide, detour))
            def _():
                one(lax.rem(col + 2, COLS), y)

            return carry

        lax.fori_loop(0, LINES, at_line, 0)

    def forward_halo():
        forward(2 - odd, 1, NEAR)
        forward(3 - 3 * odd, 1, FAR)

    boundary_sends(THEIRS)
    end_sends()
    boundary_sends(OWN)
    inner_sends(0)

    @pl.when(at_end)
    def _():
        inner_sends(1)

    fe[pl.ds(6 * odd, 2)] = jnp.zeros((2, 2, Y * R, R), F32)

    def side_copy(n):
        return pltpu.make_async_copy(side.at[n], halo_out.at[n], side_sem.at[n])

    @pl.when(tip)
    def _():
        side[...] = jnp.zeros_like(side)
        side_copy(0).start()
        side_copy(1).start()

    @pl.when(plain)
    def _():
        share(lambda rows: wait_for(recv_sem.at[THEIRS], 2, rows))
        forward(2 * odd, 2, AHEAD)
        inner_sends(1)
        share(lambda rows: wait_for(recv_sem.at[OWN], 2, rows))
        if FORWARD_STEP == 0:
            forward_halo()

    for copy in constants:
        copy.wait()

    def transform(groups):
        real = jnp.concatenate([re for re, _ in groups], axis=1)
        imag = jnp.concatenate([im for _, im in groups], axis=1)
        high, low = halves(jnp.concatenate([real, imag], axis=0))
        table = dft[...]
        section = dot(table, jnp.concatenate([high, high, low], axis=0))
        cos, sin = twist[0], twist[1]
        turned = []
        for n in range(len(groups)):
            re = section[:R, n * R : (n + 1) * R]
            im = section[R:, n * R : (n + 1) * R]
            turned.append(
                jnp.concatenate([re * cos - im * sin, re * sin + im * cos], axis=1)
            )
        high, low = halves(jnp.concatenate(turned, axis=0))
        final = dot_nt(table, jnp.concatenate([high, high, low], axis=1))
        return [
            (final[:R, n * R : (n + 1) * R], final[R:, n * R : (n + 1) * R])
            for n in range(len(groups))
        ]

    def series(slot, y):
        return tuple(rx[c, slot, pl.ds(y, R, stride=Y), :] for c in range(2))

    def plane_of(y):
        return pl.ds(pl.multiple_of(y * R, R), R)

    def own_pair(slot, where, p):
        groups_e, groups_n = [], []
        for n in range(2):
            y = 2 * p + n
            re, im = series(slot, y)
            intensity = re * re + im * im
            rate = ion_ref[y, 4 * me + where - 2] * jnp.exp(
                -BARRIER * lax.rsqrt(intensity + 1.0)
            )
            sums = dot(jnp.concatenate(halves(rate), axis=1), within[...])
            earlier = dot(before[...], jnp.concatenate(halves(sums[:, R:]), axis=0))
            plasma = 1.0 - jnp.exp(-(sums[:, :R] + earlier))
            groups_e.append((re, im))
            kerr = KERR * intensity
            groups_n.append((-kerr * im - plasma * re, kerr * re - plasma * im))
        spectra = transform(groups_e + groups_n)
        c = coupling[...]
        for n in range(2):
            at = plane_of(2 * p + n)
            e_re, e_im = spectra[n]
            n_re, n_im = spectra[2 + n]
            fe[where, 0, at, :] = e_re
            fe[where, 1, at, :] = e_im
            part[where - 2, 0, at, :] = e_re - c * n_im
            part[where - 2, 1, at, :] = e_im + c * n_re

    def halo_four(slot, where, p):
        spectra = transform([series(slot, 4 * p + y) for y in range(4)])
        for y in range(4):
            at = plane_of(4 * p + y)
            side[where, 0, at, :], side[where, 1, at, :] = spectra[y]

    def swap(i):
        where = 4 + i - 2 * odd
        return pltpu.make_async_remote_copy(
            src_ref=fe.at[where],
            dst_ref=fe.at[jnp.where(odd == 0, i, 6 + i)],
            send_sem=swap_send.at[i],
            recv_sem=swap_recv.at[i],
            device_id=(me + 1 - 2 * odd, g),
            device_id_type=MESH,
        )

    def spectrum_to_partner(n):
        return pltpu.make_async_remote_copy(
            src_ref=fe.at[jnp.where(odd == 0, 2 + n, 5 - n)],
            dst_ref=halo_out.at[n],
            send_sem=halo_send.at[n],
            recv_sem=halo_recv.at[n],
            device_id=(partner, partner_gx),
            device_id_type=MESH,
        )

    start = jnp.where(at_end, 0, BOUNDARY_STEP)

    def own_row(step, carry):
        @pl.when(jnp.logical_and(step == start, plain))
        def _():
            share(lambda rows: wait_for(recv_sem.at[AHEAD], 2, rows), of_partner=True)

        @pl.when(jnp.logical_and(step == start, at_end))
        def _():
            wait_for(recv_sem.at[OWN], 2, 1024)

        boundary = jnp.logical_and(step >= start, step < start + 2)
        i = jnp.where(boundary, step - start, jnp.where(step < start, step, step - 2))
        for n in range(2):

            @pl.when(jnp.logical_and(jnp.logical_not(boundary), i == n))
            def _(n=n):
                wait_for(recv_sem.at[INNER + n], 1, 1024)

        @pl.when(jnp.logical_and(step == FORWARD_STEP - 1, plain))
        def _():
            forward_halo()

        near_first = jnp.where(odd == 0, 2 + i, 1 - i)
        slot = jnp.where(boundary, near_first, 4 + i)
        where = jnp.where(boundary, near_first + 4 * odd, 4 + i - 2 * odd)

        def body(p, carry):
            own_pair(slot, where, p)
            return carry

        lax.fori_loop(0, Y // 2, body, 0, unroll=4)
        for n in range(2):

            @pl.when(jnp.logical_and(jnp.logical_not(boundary), i == n))
            def _(n=n):
                swap(n).start()

            @pl.when(jnp.logical_and(spectral, step == n))
            def _(n=n):
                spectrum_to_partner(n).start()

        return carry

    lax.fori_loop(0, ROWS, own_row, 0)

    def inner_terms(row):
        def block(n, carry):
            k = pl.multiple_of(n * 8, 8)
            d = diffraction[pl.ds(k, 8), :] * (1.0 / 12.0)
            lap = []
            for c in range(2):
                mid = [fe[row + 2, c, pl.ds(y * R + k, 8), :] for y in range(Y)]
                planes = []
                for y in range(Y):
                    at = pl.ds(y * R + k, 8)
                    near = fe[row + 1, c, at, :] + fe[row + 3, c, at, :]
                    far = fe[row, c, at, :] + fe[row + 4, c, at, :]
                    for o in (-1, 1):
                        if 0 <= y + o < Y:
                            near = near + mid[y + o]
                    for o in (-2, 2):
                        if 0 <= y + o < Y:
                            far = far + mid[y + o]
                    planes.append(16.0 * near - far - 60.0 * mid[y])
                lap.append(planes)
            for y in range(Y):
                at = pl.ds(y * R + k, 8)
                to = pl.ds(k * Y + y, 8, stride=Y)
                result[row, 0, to, :] = part[row, 0, at, :] - d * lap[1][y]
                result[row, 1, to, :] = part[row, 1, at, :] + d * lap[0][y]
            return carry

        lax.fori_loop(0, R // 8, block, 0)
        pltpu.make_async_copy(result.at[row], q_out.at[:, row], out_sem.at[row]).start()

    def terms_step(step, carry):
        @pl.when(step == 2)
        def _():
            for n in range(2):
                swap(n).wait_recv()

        inner_terms(jnp.where(odd == 0, step, ROWS - 1 - step))
        return carry

    lax.fori_loop(0, ROWS, terms_step, 0)

    def halo_step(n, carry):
        for i, kind in enumerate((NEAR, FAR)):

            @pl.when(n == i)
            def _(kind=kind):
                share(lambda rows: wait_for(recv_sem.at[kind], 1, rows), of_partner=True)

        slot = jnp.where(odd == 0, 1 - n, 2 + n)

        def body(p, carry):
            halo_four(slot, n, p)
            return carry

        lax.fori_loop(0, Y // 4, body, 0, unroll=2)
        side_copy(n).start()
        return carry

    @pl.when(plain)
    def _():
        lax.fori_loop(0, 2, halo_step, 0)

    for row in range(ROWS):
        pltpu.make_async_copy(result.at[row], q_out.at[:, row], out_sem.at[row]).wait()
    for n in range(2):
        swap(n).wait_send()
        wait_for(send_sem.at[INNER + n], 1, 31 * 32)
    wait_for(send_sem.at[OWN], 2, 19 * 32)

    @pl.when(plain)
    def _():
        wait_for(send_sem.at[THEIRS], 2, 11 * 32)
        share(lambda rows: wait_for(send_sem.at[AHEAD], 2, rows))
        share(lambda rows: wait_for(send_sem.at[NEAR], 1, rows))
        share(lambda rows: wait_for(send_sem.at[FAR], 1, rows))

    @pl.when(at_end)
    def _():
        wait_for(send_sem.at[THEIRS], 2, 12 * 32)

    @pl.when(spectral)
    def _():
        for n in range(2):
            spectrum_to_partner(n).wait()

    @pl.when(jnp.logical_or(plain, tip))
    def _():
        for n in range(2):
            side_copy(n).wait()


def add_halo(
    q_in, halo_in, diffraction_in, out,
    q, halo, diffraction, result, staged, q_sem, halo_sem, d_sem, out_sem, copy_sem,
):
    odd = lax.rem(lax.axis_index("ta"), 2)
    base = 2 * odd
    depth = R // PIECES

    def copies(n):
        wide = pl.ds(n * depth * Y, depth * Y)
        thin = pl.ds(n * depth, depth)
        rows = pl.ds(base, 2)
        return (
            pltpu.make_async_copy(q_in.at[:, rows, wide], q.at[:, :, wide], q_sem.at[n]),
            pltpu.make_async_copy(
                halo_in.at[:, :, :, thin], halo.at[:, :, :, thin], halo_sem.at[n]
            ),
            pltpu.make_async_copy(result.at[:, :, wide], out.at[:, rows, wide], out_sem.at[n]),
        )

    first = pltpu.make_async_copy(diffraction_in, diffraction, d_sem)
    first.start()
    for n in range(PIECES):
        for copy in copies(n)[:2]:
            copy.start()
    others = pl.ds(2 - base, 2)
    same_in = pltpu.make_async_copy(q_in.at[:, others], staged, copy_sem.at[0])
    same_out = pltpu.make_async_copy(staged, out.at[:, others], copy_sem.at[1])
    same_in.start()
    first.wait()
    for n in range(PIECES):
        for copy in copies(n)[:2]:
            copy.wait()

        def block(i, carry, n=n):
            k = pl.multiple_of(n * depth + 8 * i, 8)
            at_k = pl.ds(k, 8)
            d = diffraction[at_k, :] * (1.0 / 12.0)
            for y in range(Y):
                outer, second = [], []
                for c in range(2):
                    near, far = halo[0, c, y, at_k, :], halo[1, c, y, at_k, :]
                    outer.append(16.0 * near - far)
                    second.append(-near)
                at = pl.ds(k * Y + y, 8, stride=Y)
                for row, lap in ((odd, outer), (1 - odd, second)):
                    result[0, row, at, :] = q[0, row, at, :] - d * lap[1]
                    result[1, row, at, :] = q[1, row, at, :] + d * lap[0]
            return carry

        lax.fori_loop(0, depth // 8, block, 0)
        copies(n)[2].start()
        if n == COPY_AFTER:
            same_in.wait()
            same_out.start()
    same_out.wait()
    for n in range(PIECES):
        copies(n)[2].wait()


def on_device(field, ion_rate, diffraction, coupling):
    x_rows = field.shape[1]
    tiles = field.reshape(2, x_rows, Y, 4, R).transpose(0, 1, 3, 2, 4).reshape(2, x_rows, 32, R)
    dft, twist, within, before = tables()
    hbm = pl.BlockSpec(memory_space=pl.ANY)
    q, halo = pl.pallas_call(
        kernel,
        out_shape=[
            jax.ShapeDtypeStruct((2, ROWS, R * Y, R), F32),
            jax.ShapeDtypeStruct((2, 2, Y * R, R), F32),
        ],
        in_specs=[hbm] * 8,
        out_specs=[hbm, hbm],
        scratch_shapes=[
            pltpu.VMEM((2, ROWS + 2, R * Y, R), F32),
            pltpu.VMEM((ROWS + 4, 2, Y * R, R), F32),
            pltpu.VMEM((ROWS, 2, Y * R, R), F32),
            pltpu.VMEM((ROWS, 2, R * Y, R), F32),
            pltpu.VMEM((2, 2, Y * R, R), F32),
            pltpu.SMEM((Y, x_rows), F32),
            pltpu.VMEM((R, R), F32),
            pltpu.VMEM((R, R), F32),
            pltpu.VMEM(dft.shape, BF16),
            pltpu.VMEM(twist.shape, F32),
            pltpu.VMEM(within.shape, BF16),
            pltpu.VMEM(before.shape, BF16),
            pltpu.SemaphoreType.DMA((7,)),
            pltpu.SemaphoreType.DMA((7,)),
            pltpu.SemaphoreType.DMA((7,)),
            pltpu.SemaphoreType.DMA((2,)),
            pltpu.SemaphoreType.DMA((2,)),
            pltpu.SemaphoreType.DMA((2,)),
            pltpu.SemaphoreType.DMA((2,)),
            pltpu.SemaphoreType.DMA((2,)),
            pltpu.SemaphoreType.DMA((ROWS,)),
        ],
        compiler_params=pltpu.CompilerParams(
            collective_id=0, has_side_effects=True, vmem_limit_bytes=60 * 1024 * 1024
        ),
    )(
        ion_rate.T,
        tiles,
        coupling.reshape(R, R),
        diffraction.reshape(R, R),
        jnp.asarray(dft),
        jnp.asarray(twist),
        jnp.asarray(within),
        jnp.asarray(before),
    )
    spectrum = pl.pallas_call(
        add_halo,
        out_shape=jax.ShapeDtypeStruct((2, ROWS, R * Y, R), F32),
        in_specs=[hbm] * 3,
        out_specs=hbm,
        scratch_shapes=[
            pltpu.VMEM((2, 2, R * Y, R), F32),
            pltpu.VMEM((2, 2, Y, R, R), F32),
            pltpu.VMEM((R, R), F32),
            pltpu.VMEM((2, 2, R * Y, R), F32),
            pltpu.VMEM((2, 2, R * Y, R), F32),
            pltpu.SemaphoreType.DMA((PIECES,)),
            pltpu.SemaphoreType.DMA((PIECES,)),
            pltpu.SemaphoreType.DMA,
            pltpu.SemaphoreType.DMA((PIECES,)),
            pltpu.SemaphoreType.DMA((2,)),
        ],
        compiler_params=pltpu.CompilerParams(vmem_limit_bytes=60 * 1024 * 1024),
    )(q, halo.reshape(2, 2, Y, R, R), diffraction.reshape(R, R))
    spectrum = spectrum.reshape(2, ROWS, R, Y, R).transpose(0, 1, 3, 2, 4)
    return spectrum.reshape(2, ROWS, Y, R * R)


def solution(mesh):
    in_specs = (P(None, "gx", None, "ta"), P("gx", None), P(), P())
    out_specs = P(None, ("gx", "ta"), None, None)
    return jax.shard_map(
        on_device, mesh=mesh, in_specs=in_specs, out_specs=out_specs, check_vma=False
    )
```

time: 84.8 us -> 83.4 us (0.983)
  Pallas kernels: 84.7 us -> 82.6 us
    pallas_call x1, Pallas kernels: 79.3 us -> 77.5 us  [on_device(): pl.pallas_call(kernel, out_shape=[jax.ShapeDtypeStruct((2, ROWS, R * Y, R...]
where the time goes in v4:
time: 83.4 us; the launch traced here: 82.6 us
  Pallas kernels  82.6 us (99%)
    pallas_call x1, Pallas kernels, on_device(): pl.pallas_call(kernel, out_shape=[jax.ShapeDtypeStruct((2, ROWS, R * Y, R...  77.5 us
    pallas_call x1, Pallas kernels, on_device(): pl.pallas_call(add_halo, out_shape=jax.ShapeDtypeStruct((2, ROWS, R * Y,...  5.09 us

profile of v4, /device:TPU:96, one launch (start us, length us, event | category | flops | bytes accessed | tf_op | source)
XLA Modules:
  0.0 82.6 jit_solution(7322794184225088568)
XLA Ops:
  0.0 77.5 %shard_map.82 = (f32[2,4,1024,128]{3,2,1,0:T(8,128)}, f32[2,2,1024,128]{3,2,1,0:T(8,128)}) custom-call(f32[8,128]{1,0:T(8,128)} %bitcast.19, f32[2,128,32,128]{3,2,1,0:T(8,128)} %bitcast.14, f32[128,128]{1,0:T(8,128)} %bitcast.18, f32[128,128]{1,0:T(8,128)} %bitcast.16, bf16[256,768]{1,0:T(8,128)(2,1)} %constant.8.clone.dft_in, ...), custom_call_target="tpu_custom_call" | custom-call | tf_op jit(solution)/shard_map/pallas_call | solution.py:579
  77.5 5.1 %shard_map.83 = f32[2,4,1024,128]{3,2,1,0:T(8,128)} custom-call(f32[2,4,1024,128]{3,2,1,0:T(8,128)} %get-tuple-element.7.q_in, f32[2,2,8,128,128]{4,3,2,1,0:T(8,128)} %bitcast.15, f32[128,128]{1,0:T(8,128)} %bitcast.17), custom_call_target="tpu_custom_call" | custom-call | tf_op jit(solution)/shard_map/pallas_call | solution.py:623

commit v5 on v4

--- a/solution.py
+++ b/solution.py
@@ -23,9 +23,9 @@
 INNER, THEIRS, OWN, AHEAD, NEAR, FAR = 0, 2, 3, 4, 5, 6
 BOUNDARY_STEP = 1
 FORWARD_STEP = 2
-DETOUR = (2,)
+DETOUR = (0,)
 COPY_AFTER = 1
-PIECES = 4
+PIECES = 2
 F32 = jnp.float32
 BF16 = jnp.bfloat16
 
@@ -262,8 +262,8 @@
         forward(2 - odd, 1, NEAR)
         forward(3 - 3 * odd, 1, FAR)
 
+    end_sends()
     boundary_sends(THEIRS)
-    end_sends()
     boundary_sends(OWN)
     inner_sends(0)
 

time: 83.4 us -> 81.5 us (0.977)
  Pallas kernels: 82.6 us -> 81.3 us
where the time goes in v5:
time: 81.5 us; the launch traced here: 81.3 us
  Pallas kernels  81.3 us (100%)
    pallas_call x1, Pallas kernels, on_device(): pl.pallas_call(kernel, out_shape=[jax.ShapeDtypeStruct((2, ROWS, R * Y, R...  77 us
    pallas_call x1, Pallas kernels, on_device(): pl.pallas_call(add_halo, out_shape=jax.ShapeDtypeStruct((2, ROWS, R * Y,...  4.34 us

profile of v5, /device:TPU:96, one launch (start us, length us, event | category | flops | bytes accessed | tf_op | source)
XLA Modules:
  0.0 81.3 jit_solution(17869595713951640130)
XLA Ops:
  0.0 77.0 %shard_map.82 = (f32[2,4,1024,128]{3,2,1,0:T(8,128)}, f32[2,2,1024,128]{3,2,1,0:T(8,128)}) custom-call(f32[8,128]{1,0:T(8,128)} %bitcast.19, f32[2,128,32,128]{3,2,1,0:T(8,128)} %bitcast.14, f32[128,128]{1,0:T(8,128)} %bitcast.18, f32[128,128]{1,0:T(8,128)} %bitcast.16, bf16[256,768]{1,0:T(8,128)(2,1)} %constant.8.clone.dft_in, ...), custom_call_target="tpu_custom_call" | custom-call | tf_op jit(solution)/shard_map/pallas_call | solution.py:579
  77.0 4.3 %shard_map.83 = f32[2,4,1024,128]{3,2,1,0:T(8,128)} custom-call(f32[2,4,1024,128]{3,2,1,0:T(8,128)} %get-tuple-element.7.q_in, f32[2,2,8,128,128]{4,3,2,1,0:T(8,128)} %bitcast.15, f32[128,128]{1,0:T(8,128)} %bitcast.17), custom_call_target="tpu_custom_call" | custom-call | tf_op jit(solution)/shard_map/pallas_call | solution.py:623

commit v6 on v5

--- a/solution.py
+++ b/solution.py
@@ -22,9 +22,9 @@
 COLS = 4
 INNER, THEIRS, OWN, AHEAD, NEAR, FAR = 0, 2, 3, 4, 5, 6
 BOUNDARY_STEP = 1
-FORWARD_STEP = 2
+FORWARD_STEP = 0
 DETOUR = (0,)
-COPY_AFTER = 1
+COPY_AFTER = 0
 PIECES = 2
 F32 = jnp.float32
 BF16 = jnp.bfloat16
@@ -533,13 +533,14 @@
 
     first = pltpu.make_async_copy(diffraction_in, diffraction, d_sem)
     first.start()
+    others = pl.ds(2 - base, 2)
+    same_in = pltpu.make_async_copy(q_in.at[:, others], staged, copy_sem.at[0])
+    same_out = pltpu.make_async_copy(staged, out.at[:, others], copy_sem.at[1])
     for n in range(PIECES):
         for copy in copies(n)[:2]:
             copy.start()
-    others = pl.ds(2 - base, 2)
-    same_in = pltpu.make_async_copy(q_in.at[:, others], staged, copy_sem.at[0])
-    same_out = pltpu.make_async_copy(staged, out.at[:, others], copy_sem.at[1])
-    same_in.start()
+        if n == COPY_AFTER:
+            same_in.start()
     first.wait()
     for n in range(PIECES):
         for copy in copies(n)[:2]:

time: 81.5 us -> 81.4 us (level)
  no operation moved by 1% of the time
where the time goes in v6:
time: 81.4 us; the launch traced here: 81.3 us
  Pallas kernels  81.3 us (100%)
    pallas_call x1, Pallas kernels, on_device(): pl.pallas_call(kernel, out_shape=[jax.ShapeDtypeStruct((2, ROWS, R * Y, R...  77 us
    pallas_call x1, Pallas kernels, on_device(): pl.pallas_call(add_halo, out_shape=jax.ShapeDtypeStruct((2, ROWS, R * Y,...  4.26 us

profile of v6, /device:TPU:96, one launch (start us, length us, event | category | flops | bytes accessed | tf_op | source)
XLA Modules:
  0.0 81.3 jit_solution(875004374710040045)
XLA Ops:
  0.0 77.0 %shard_map.82 = (f32[2,4,1024,128]{3,2,1,0:T(8,128)}, f32[2,2,1024,128]{3,2,1,0:T(8,128)}) custom-call(f32[8,128]{1,0:T(8,128)} %bitcast.19, f32[2,128,32,128]{3,2,1,0:T(8,128)} %bitcast.14, f32[128,128]{1,0:T(8,128)} %bitcast.18, f32[128,128]{1,0:T(8,128)} %bitcast.16, bf16[256,768]{1,0:T(8,128)(2,1)} %constant.8.clone.dft_in, ...), custom_call_target="tpu_custom_call" | custom-call | tf_op jit(solution)/shard_map/pallas_call | solution.py:580
  77.0 4.3 %shard_map.83 = f32[2,4,1024,128]{3,2,1,0:T(8,128)} custom-call(f32[2,4,1024,128]{3,2,1,0:T(8,128)} %get-tuple-element.7.q_in, f32[2,2,8,128,128]{4,3,2,1,0:T(8,128)} %bitcast.15, f32[128,128]{1,0:T(8,128)} %bitcast.17), custom_call_target="tpu_custom_call" | custom-call | tf_op jit(solution)/shard_map/pallas_call | solution.py:624
